TPU v7x, 32 devices: a whole 2x2x4 slice. The times are simulated.
32 devices in a mesh: ctx: 16 (over z, y, core), wa: 2 (over x).
Axes of the slice: x: 2, y: 2, z: 4, core: 2. Of those that a mesh axis runs over, the one named last changes fastest.
Arguments:
- tokens: bfloat16 [4, 4096, 768], P('wa', 'ctx'), may hold values from -6 to 6
- teacher: bfloat16 [4, 4096, 768], P('wa', 'ctx'), may hold values from -12 to 12
- lengths: int32 [4], P('wa'), may hold values from 1024 to 4096, as said below
- block_order: int32 [32], replicated, may hold values from 0 to 31, each once
- query_weight: bfloat16 [768, 768], P('wa'), may hold values from -0.21875 to 0.21875
- query_bias: bfloat16 [768], P('wa'), may hold values from -1.796875 to 1.796875
- key_weight: bfloat16 [768, 768], P('wa'), may hold values from -0.21875 to 0.21875
- value_weight: bfloat16 [768, 768], P('wa'), may hold values from -0.21875 to 0.21875
- value_bias: bfloat16 [768], P('wa'), may hold values from -0.059814453 to 0.059814453
- out_weight: bfloat16 [768, 768], P('wa'), may hold values from -12 to 12
- out_bias: bfloat16 [768], P('wa'), may hold values from -1.796875 to 1.796875
- gain_one: bfloat16 [768], P('wa'), may hold values from 0.5 to 1.5
- shift_one: bfloat16 [768], P('wa'), may hold values from -1.796875 to 1.796875
- inner_weight: bfloat16 [768, 3072], P('wa'), may hold values from -0.21875 to 0.21875
- inner_bias: bfloat16 [3072], P('wa'), may hold values from -1.796875 to 1.796875
- outer_weight: bfloat16 [3072, 768], P('wa'), may hold values from -0.109375 to 0.109375
- outer_bias: bfloat16 [768], P('wa'), may hold values from -1.796875 to 1.796875
- gain_two: bfloat16 [768], P('wa'), may hold values from 0.5 to 1.5
- shift_two: bfloat16 [768], P('wa'), may hold values from -1.796875 to 1.796875
Outputs:
- output: bfloat16 [4, 4096, 768], P('wa', 'ctx')
- tokens_grad: float32 [4, 4096, 768], P('wa', 'ctx')
- query_weight_grad: float32 [768, 768], P('wa')
- query_bias_grad: float32 [768], P('wa')
- key_weight_grad: float32 [768, 768], P('wa')
- value_weight_grad: float32 [768, 768], P('wa')
- value_bias_grad: float32 [768], P('wa')
- out_weight_grad: float32 [768, 768], P('wa')
- out_bias_grad: float32 [768], P('wa')
- gain_one_grad: float32 [768], P('wa')
- shift_one_grad: float32 [768], P('wa')
- inner_weight_grad: float32 [768, 3072], P('wa')
- inner_bias_grad: float32 [3072], P('wa')
- outer_weight_grad: float32 [3072, 768], P('wa')
- outer_bias_grad: float32 [768], P('wa')
- gain_two_grad: float32 [768], P('wa')
- shift_two_grad: float32 [768], P('wa')
- loss: float32 [], replicated
Inputs may be any that keep to these rules, and one draw needn't show every extreme that they name: `lengths`: one sequence of every draw fills all 4096 slots. `block_order`: every block number appears once.
All inputs are finite; a program needn't handle non-finite values.
Results may differ from a plain program's by a relative error of at most 0.017.
Values may be sent and summed in bfloat16 or wider, within the bound.
A program may use at most 384 MiB of HBM per device.

v0:
```python
import functools
import math

import jax
import jax.numpy as jnp
from jax import lax
from jax.experimental import pallas as pl
from jax.experimental.pallas import tpu as pltpu
from jax.sharding import PartitionSpec as P

DH = 64
BLK = 128
GROUPS = 4
LN2 = math.log(2.0)
NT = (((1,), (1,)), ((), ()))
NN = (((1,), (0,)), ((), ()))
TN = (((0,), (0,)), ((), ()))
F32 = jnp.float32
BF16 = jnp.bfloat16
VMEM = pl.BlockSpec(memory_space=pltpu.VMEM)
SMEM = pl.BlockSpec(memory_space=pltpu.SMEM)
ANY = pl.BlockSpec(memory_space=pl.ANY)
ROOM = pltpu.CompilerParams(vmem_limit_bytes=62 * 2**20)


def dot(left, right, dims=NN):
    return lax.dot_general(left, right, dims, preferred_element_type=F32)


def cost(us):
    return pl.CostEstimate(flops=int(us * 1.15e9), bytes_accessed=1 << 20, transcendentals=0)


def weight_copies(full, own, first, second, sems, base):
    x, c = lax.axis_index("wa"), lax.rem(lax.axis_index("ctx"), 2)
    half = own.shape[0]
    quarter = half // 2
    other = (1 - x) * half
    places = (
        (own, x * half, half),
        (first, other + c * quarter, quarter),
        (second, other + (1 - c) * quarter, quarter),
    )
    return [
        pltpu.make_async_copy(
            src, full.at[pl.ds(pl.multiple_of(start, quarter), size)], sems.at[base + i]
        )
        for i, (src, start, size) in enumerate(places)
    ]


class Counts:
    def __init__(self, lengths, order):
        self.lengths, self.order = lengths, order

    def __getitem__(self, i):
        place = 2 * lax.axis_index("ctx") + i % 2
        return self.lengths[i // 2] - self.order[place] * BLK


def valid_rows(sc, s, rows):
    row = lax.broadcasted_iota(jnp.int32, (rows, 1), 0)
    first = jnp.where(row < sc[2 * s], 1.0, 0.0)
    later = jnp.where(row - BLK < sc[2 * s + 1], 1.0, 0.0)
    return jnp.where(row < BLK, first, later)


def half_copies(full, own, other, sems, base):
    x, half = lax.axis_index("wa"), own.shape[0]
    return [
        pltpu.make_async_copy(
            src, full.at[pl.ds(pl.multiple_of(k * half, half), half)], sems.at[base + i]
        )
        for i, (src, k) in enumerate(((own, x), (other, 1 - x)))
    ]


def project_kernel(sc, tok, vec, wq, wk, wv, first, second, *rest):
    seqs, rows, width = tok.shape
    outs, (full, sems) = rest[: 2 * seqs], rest[2 * seqs :]
    quarter = wq.shape[0] // 2
    copies = []
    for i, own in enumerate((wq, wk, wv)):
        part = pl.ds(i * quarter, quarter)
        copies.append(
            weight_copies(full.at[i], own, first.at[part], second.at[part], sems, 3 * i)
        )
    for group in copies:
        for copy in group:
            copy.start()
    flat = tok[...].reshape(seqs * rows, width)
    per = width // GROUPS
    heads = per // DH
    valid = jnp.concatenate([valid_rows(sc, s, rows) for s in range(seqs)], 0) > 0.0
    for copy in copies[1]:
        copy.wait()
    keys = jnp.where(valid, dot(flat, full[1]), 0.0).astype(BF16)
    for copy in copies[2]:
        copy.wait()
    values = jnp.where(valid, dot(flat, full[2]) + vec[1:2, :], 0.0).astype(BF16)
    for s in range(seqs):
        rs = slice(s * rows, (s + 1) * rows)
        for g in range(GROUPS):
            for h in range(heads):
                cols = slice(g * per + h * DH, g * per + (h + 1) * DH)
                outs[2 * s + 1][g, :, h * 128 : (h + 1) * 128] = jnp.concatenate(
                    [keys[rs, cols], values[rs, cols]], 1
                )
    for copy in copies[0]:
        copy.wait()
    queries = ((dot(flat, full[0]) + vec[0:1, :]) * (DH**-0.5 / LN2)).astype(BF16)
    for s in range(seqs):
        rs = slice(s * rows, (s + 1) * rows)
        for g in range(GROUPS):
            outs[2 * s][g] = queries[rs, g * per : (g + 1) * per]


def project(sc, tok, vec, wq, wk, wv, first, second):
    seqs, rows, width = tok.shape
    per = width // GROUPS
    shapes = [
        jax.ShapeDtypeStruct((GROUPS, rows, n), BF16) for _ in range(seqs) for n in (per, 2 * per)
    ]
    return pl.pallas_call(
        project_kernel,
        out_shape=shapes,
        in_specs=[SMEM, VMEM, VMEM] + [ANY] * 5,
        out_specs=[VMEM] * len(shapes),
        scratch_shapes=[pltpu.VMEM((3, width, width), BF16), pltpu.SemaphoreType.DMA((9,))],
        compiler_params=ROOM,
        cost_estimate=cost(5),
        name="project",
    )(sc, tok, vec, wq, wk, wv, first, second)


def load_pieces(pieces, kv, sems):
    per = pieces[0].shape[0]
    copies = [
        pltpu.make_async_copy(piece, kv.at[pl.ds(i * per, per)], sems.at[i])
        for i, piece in enumerate(pieces)
    ]
    for copy in copies:
        copy.start()
    for copy in copies:
        copy.wait()


def forward_kernel(wide, narrow, count, s, per_plane, lengths, order, q_ref, *rest):
    pieces, rest = rest[:count], rest[count:]
    o_ref, lse_ref, kv_ref, qa, acc, sums, spots, sems = rest
    blocks = q_ref.shape[0]
    heads = q_ref.shape[2] // DH
    rows = blocks * BLK
    length = lengths[s]
    place = lax.rem(lax.axis_index("ctx"), per_plane)

    def put(b, _):
        owner = b // 2
        offset = lax.bitwise_xor(lax.rem(owner, per_plane), place)
        piece = 0
        for bit in range(per_plane.bit_length() - 1):
            piece = 2 * piece + lax.rem(lax.div(offset, 1 << bit), 2)
        spots[order[b]] = (piece * GROUPS + lax.div(owner, per_plane)) * 2 + lax.rem(b, 2)
        return 0

    lax.fori_loop(0, order.shape[0], put, 0)
    load_pieces(pieces, kv_ref, sems)

    def gather(h, start, n):
        return jnp.concatenate(
            [kv_ref[spots[start + i], :, h * 128 : (h + 1) * 128] for i in range(n)], 0
        )

    whole = length // (wide * BLK)
    tail = whole * wide
    tails = (length - tail * BLK + narrow * BLK - 1) // (narrow * BLK)
    for h in range(heads):
        hs = slice(h * DH, (h + 1) * DH)
        own = jnp.concatenate([q_ref[b, :, hs] for b in range(blocks)], 0)
        qa[...] = jnp.concatenate([own, jnp.zeros_like(own)], 1)
        acc[...] = jnp.zeros_like(acc)
        sums[...] = jnp.zeros_like(sums)

        def step(start, n, masked, h=h):
            kv = gather(h, start, n)
            scores = dot(qa[...], kv, NT)
            if masked:
                place = lax.broadcasted_iota(jnp.int32, scores.shape, 1) + start * BLK
                scores = jnp.where(place < length, scores, -1e30)
            p = jnp.exp2(scores)
            sums[...] += sum(p[:, i * 128 : (i + 1) * 128] for i in range(n))
            acc[...] += dot(p.astype(BF16), kv)

        def wide_step(j, _, step=step):
            step(j * wide, wide, False)
            return 0

        def narrow_step(j, _, step=step):
            step(tail + j * narrow, narrow, True)
            return 0

        lax.fori_loop(0, whole, wide_step, 0)
        lax.fori_loop(0, tails, narrow_step, 0)
        total = jnp.sum(sums[...], 1, keepdims=True)
        across = jnp.transpose(jnp.broadcast_to(total, (rows, 128)))[:8]
        good = (jnp.min(across) > 2.0**-80) & (jnp.max(across) < 2.0**100)

        @pl.when(good)
        def _(h=h, hs=hs, total=total, across=across):
            lse_ref[h] = jnp.log2(across)
            o_ref[:, hs] = (acc[:, DH:] * (1.0 / total)).astype(BF16)

        @pl.when(jnp.logical_not(good))
        def _(h=h, hs=hs):
            key_blocks = (length + BLK - 1) // BLK

            def rows_step(t, _):
                part = pl.ds(pl.multiple_of(t * BLK, BLK), BLK)
                q = qa[part, :]

                def scores_of(j):
                    kv = gather(h, j, 1)
                    scores = dot(q, kv, NT)
                    place = lax.broadcasted_iota(jnp.int32, scores.shape, 1) + j * BLK
                    return kv, jnp.where(place < length, scores, -1e30)

                largest = lax.fori_loop(
                    0,
                    key_blocks,
                    lambda j, m: jnp.maximum(m, jnp.max(scores_of(j)[1], 1, keepdims=True)),
                    jnp.full((BLK, 1), -1e30, F32),
                )
                acc[part, :] = jnp.zeros((BLK, 128), F32)
                sums[part, :] = jnp.zeros((BLK, 128), F32)

                def add(j, _):
                    kv, scores = scores_of(j)
                    p = jnp.exp2(scores - largest)
                    sums[part, :] += p
                    acc[part, :] += dot(p.astype(BF16), kv)
                    return 0

                lax.fori_loop(0, key_blocks, add, 0)
                row_total = jnp.sum(sums[part, :], 1, keepdims=True)
                lse = largest + jnp.log2(row_total)
                lse_ref[h, :, part] = jnp.transpose(jnp.broadcast_to(lse, (BLK, 128)))[:8]
                o_ref[part, hs] = (acc[part, :][:, DH:] * (1.0 / row_total)).astype(BF16)
                return 0

            lax.fori_loop(0, rows // BLK, rows_step, 0)


def attend(s, per_plane, lengths, order, q, pieces):
    blocks, _, per = q.shape
    rows, heads = blocks * BLK, per // DH
    key_blocks = len(pieces) * pieces[0].shape[0]
    return pl.pallas_call(
        functools.partial(forward_kernel, 8, 2, len(pieces), s, per_plane),
        out_shape=(
            jax.ShapeDtypeStruct((rows, per), BF16),
            jax.ShapeDtypeStruct((heads, 8, rows), F32),
        ),
        in_specs=[SMEM, SMEM, VMEM] + [ANY] * len(pieces),
        out_specs=(VMEM, VMEM),
        scratch_shapes=[
            pltpu.VMEM((key_blocks, BLK, 2 * per), BF16),
            pltpu.VMEM((rows, 128), BF16),
            pltpu.VMEM((rows, 128), F32),
            pltpu.VMEM((rows, 128), F32),
            pltpu.SMEM((key_blocks,), jnp.int32),
            pltpu.SemaphoreType.DMA((len(pieces),)),
        ],
        compiler_params=ROOM,
        cost_estimate=cost(20),
        name="attend",
    )(lengths, order, q, *pieces)


def backward_kernel(qn, kn, count, sc, q_ref, do_ref, o_ref, lse_ref, *rest):
    pieces, dq_ref, outs = rest[:count], rest[count], rest[count + 1 : 2 * count + 1]
    kv_ref, both, dkv, dq, lse_row, delta_row, sems = rest[2 * count + 1 :]
    blocks = q_ref.shape[0]
    heads = q_ref.shape[2] // DH
    key_blocks = kv_ref.shape[0]
    tile = qn * BLK
    length, used = sc[0], sc[1]
    whole = length // (kn * BLK)
    parts = (length + kn * BLK - 1) // (kn * BLK)
    tiles = (used + qn - 1) // qn
    ones = jnp.ones((8, DH), BF16)
    load_pieces(pieces, kv_ref, sems)
    for h in range(heads):
        hs = slice(h * DH, (h + 1) * DH)

        def clear(i, _):
            dkv[pl.ds(pl.multiple_of(i * 1024, 1024), 1024), :] = jnp.zeros((1024, 128), F32)
            return 0

        lax.fori_loop(0, key_blocks // 8, clear, 0)
        dq[...] = jnp.zeros_like(dq)

        def prepare(t, _, h=h, hs=hs):
            base = pl.multiple_of(t * (2 * tile), 2 * tile)
            start = pl.multiple_of(t * tile, tile)
            places = [sc[8 + t * qn + i] for i in range(qn)]
            q = jnp.concatenate([q_ref[s, :, hs] for s in places], 0)
            do = jnp.concatenate([do_ref[s, :, hs] for s in places], 0)
            o = jnp.concatenate([o_ref[s, :, hs] for s in places], 0)
            zero = jnp.zeros_like(q)
            both[pl.ds(base, tile), :] = jnp.concatenate([q, zero], 1)
            both[pl.ds(base + tile, tile), :] = jnp.concatenate([zero, do], 1)
            product = do.astype(F32) * o.astype(F32)
            high = product.astype(BF16)
            rest_of = (product - high.astype(F32)).astype(BF16)
            delta_row[:, pl.ds(start, tile)] = dot(ones, high, NT) + dot(ones, rest_of, NT)
            lse_row[:, pl.ds(start, tile)] = jnp.concatenate(
                [lse_ref[h, :, pl.ds(pl.multiple_of(s * BLK, BLK), BLK)] for s in places], 1
            )
            return 0

        lax.fori_loop(0, tiles, prepare, 0)

        def rows_step(t, _, h=h):
            base = pl.multiple_of(t * (2 * tile), 2 * tile)
            span = pl.ds(pl.multiple_of(t * tile, tile), tile)

            def step(j, masked):
                places = [sc[8 + blocks + j * kn + i] for i in range(kn)]
                kv = jnp.concatenate([kv_ref[s, :, h * 128 : (h + 1) * 128] for s in places], 0)
                b = both[pl.ds(base, 2 * tile), :]
                found = dot(kv, b, NT)
                p = jnp.exp2(found[:, :tile] - lse_row[:1, span])
                if masked:
                    place = lax.broadcasted_iota(jnp.int32, p.shape, 0) + j * (kn * BLK)
                    p = jnp.where(place < length, p, 0.0)
                ds = (p * (found[:, tile:] - delta_row[:1, span])).astype(BF16)
                grads = dot(jnp.concatenate([ds, p.astype(BF16)], 1), b)
                for i, s in enumerate(places):
                    dkv[pl.ds(pl.multiple_of(s * BLK, BLK), BLK), :] += grads[
                        i * BLK : (i + 1) * BLK
                    ]
                dq[span, :] += dot(ds, kv, TN)

            def whole_step(j, _):
                step(j, False)
                return 0

            lax.fori_loop(0, whole, whole_step, 0)

            @pl.when(parts > whole)
            def _():
                step(whole, True)

            return 0

        lax.fori_loop(0, tiles, rows_step, 0)
        for i in range(blocks):
            dq_ref[sc[8 + i], :, hs] = (
                dq[i * BLK : (i + 1) * BLK, :DH] * DH**-0.5
            ).astype(BF16)
        level = jnp.where(lax.broadcasted_iota(jnp.int32, (1, 128), 1) < DH, LN2, 1.0)
        per_piece = key_blocks // count
        for n, out in enumerate(outs):
            for i in range(per_piece):
                b = n * per_piece + i
                out[i, :, h * 128 : (h + 1) * 128] = (
                    dkv[b * BLK : (b + 1) * BLK, :] * level
                ).astype(BF16)


def attend_back(sc, q, do, o, lse, pieces):
    blocks, _, per = q.shape
    rows = blocks * BLK
    key_blocks = len(pieces) * pieces[0].shape[0]
    return pl.pallas_call(
        functools.partial(backward_kernel, 4, 4, len(pieces)),
        out_shape=[jax.ShapeDtypeStruct(q.shape, BF16)]
        + [jax.ShapeDtypeStruct(p.shape, BF16) for p in pieces],
        in_specs=[SMEM] + [VMEM] * 4 + [ANY] * len(pieces),
        out_specs=[VMEM] * (1 + len(pieces)),
        scratch_shapes=[
            pltpu.VMEM((key_blocks, BLK, 2 * per), BF16),
            pltpu.VMEM((2 * rows, 128), BF16),
            pltpu.VMEM((key_blocks * BLK, 128), F32),
            pltpu.VMEM((rows, 128), F32),
            pltpu.VMEM((8, rows), F32),
            pltpu.VMEM((8, rows), F32),
            pltpu.SemaphoreType.DMA((len(pieces),)),
        ],
        compiler_params=ROOM,
        cost_estimate=cost(45),
        name="attend_back",
    )(sc, q, do, o, lse, *pieces)


def norm(values):
    centered = values - jnp.mean(values, -1, keepdims=True)
    inverse = lax.rsqrt(jnp.mean(centered * centered, -1, keepdims=True) + 1e-6)
    return centered * inverse, inverse


def norm_back(upstream, normed, inverse):
    return inverse * (
        upstream
        - jnp.mean(upstream, -1, keepdims=True)
        - normed * jnp.mean(upstream * normed, -1, keepdims=True)
    )


def normal_parts(x):
    z = jnp.abs(x) * (0.5**0.5)
    bell = jnp.exp(-0.5 * x * x)
    t = 1.0 / (1.0 + 0.3275911 * z)
    poly = t * (
        0.254829592
        + t * (-0.284496736 + t * (1.421413741 + t * (-1.453152027 + t * 1.061405429)))
    )
    upper = 0.5 * poly * bell
    return jnp.where(x >= 0, 1.0 - upper, upper), bell * (2.0 * math.pi) ** -0.5


def dense_kernel(sc, att4, tok, teach, vec, wide_vec, *rest):
    weights, rest = rest[:9], rest[9:]
    outs, (wo, wi, wu, slope, sems) = rest[:11], rest[11:]
    out, fg, ag, att_o, br_o, hl_o, il_o, act_o, ol_o, sums, wide_sums = outs
    rows, width = tok.shape
    hidden = wi.shape[1]
    tile = 512
    copies = [
        weight_copies(full, *weights[3 * i : 3 * i + 3], sems, 3 * i)
        for i, full in enumerate((wo, wi, wu))
    ]
    for group in copies:
        for copy in group:
            copy.start()
    per = att4.shape[2]
    att = jnp.concatenate([att4[g] for g in range(GROUPS)], 1)
    att_o[...] = att
    row = lax.broadcasted_iota(jnp.int32, (rows, 1), 0)
    mask = jnp.where(
        row < BLK, jnp.where(row < sc[0], 1.0, 0.0), jnp.where(row - BLK < sc[1], 1.0, 0.0)
    )
    out_bias, gain_one, shift_one = vec[0:1, :], vec[1:2, :], vec[2:3, :]
    outer_bias, gain_two, shift_two = vec[3:4, :], vec[4:5, :], vec[5:6, :]
    for copy in copies[0]:
        copy.wait()
    first = tok[...].astype(F32) + dot(att, wo[...]) + out_bias
    normed_one, inverse_one = norm(first)
    hidden_in = normed_one * gain_one + shift_one
    hl = hidden_in.astype(BF16)
    hl_o[...] = hl
    for copy in copies[1] + copies[2]:
        copy.wait()
    second = hidden_in + outer_bias
    for n in range(hidden // tile):
        cols = slice(n * tile, (n + 1) * tile)
        inner = dot(hl, wi[:, cols]) + wide_vec[0:1, cols]
        below, density = normal_parts(inner)
        act = (inner * below).astype(BF16)
        act_o[:, cols] = act
        slope[:, cols] = below + inner * density
        second += dot(act, wu[cols, :])
    normed_two, inverse_two = norm(second)
    final = normed_two * gain_two + shift_two
    out[...] = final.astype(BF16)
    residue = (final - teach[...].astype(F32)) * mask
    add = functools.partial(jnp.sum, axis=0, keepdims=True)
    second_grad = norm_back(residue * gain_two, normed_two, inverse_two)
    ol = second_grad.astype(BF16)
    ol_o[...] = ol
    hidden_grad = second_grad
    for n in range(hidden // tile):
        cols = slice(n * tile, (n + 1) * tile)
        il = (dot(ol, wu[cols, :], NT) * slope[:, cols]).astype(BF16)
        il_o[:, cols] = il
        wide_sums[0:1, cols] = add(il.astype(F32))
        hidden_grad += dot(il, wi[:, cols], NT)
    first_grad = norm_back(hidden_grad * gain_one, normed_one, inverse_one)
    fg[...] = first_grad
    br = first_grad.astype(BF16)
    br_o[...] = br
    att_grad = dot(br, wo[...], NT).astype(BF16)
    for g in range(GROUPS):
        ag[g] = att_grad[:, g * per : (g + 1) * per]
    sums[0:1, :] = add(residue * normed_two)
    sums[1:2, :] = add(residue)
    sums[2:3, :] = add(ol.astype(F32))
    sums[3:4, :] = add(hidden_grad * normed_one)
    sums[4:5, :] = add(hidden_grad)
    sums[5:6, :] = add(br.astype(F32))
    sums[6:7, :] = add(residue * residue)
    sums[7:8, :] = jnp.zeros((1, width), F32)


def dense(sc, att4, tok, teach, vec, wide_vec, weights):
    rows, width = tok.shape
    hidden = wide_vec.shape[1]
    narrow = jax.ShapeDtypeStruct((rows, width), BF16)
    wide = jax.ShapeDtypeStruct((rows, hidden), BF16)
    return pl.pallas_call(
        dense_kernel,
        out_shape=[
            narrow,
            jax.ShapeDtypeStruct((rows, width), F32),
            jax.ShapeDtypeStruct(att4.shape, BF16),
            narrow,
            narrow,
            narrow,
            wide,
            wide,
            narrow,
            jax.ShapeDtypeStruct((8, width), F32),
            jax.ShapeDtypeStruct((1, hidden), F32),
        ],
        in_specs=[SMEM] + [VMEM] * 5 + [ANY] * 9,
        out_specs=[VMEM] * 11,
        scratch_shapes=[
            pltpu.VMEM((width, width), BF16),
            pltpu.VMEM((width, hidden), BF16),
            pltpu.VMEM((hidden, width), BF16),
            pltpu.VMEM((rows, hidden), F32),
            pltpu.SemaphoreType.DMA((9,)),
        ],
        compiler_params=ROOM,
        cost_estimate=cost(15),
        name="dense",
    )(sc, att4, tok, teach, vec, wide_vec, *weights)


def dense_grads_kernel(seqs, *refs):
    ins, (g_out, g_inner, g_outer) = refs[: 6 * seqs], refs[6 * seqs :]
    att, br, hl, il, act, ol = (
        jnp.concatenate([ins[6 * s + i][...] for s in range(seqs)], 0) for i in range(6)
    )
    for target, left, right in ((g_out, att, br), (g_inner, hl, il), (g_outer, act, ol)):
        rows = target.shape[1]
        for n in range(4):
            piece = left[:, n * rows : (n + 1) * rows]
            for t in range(right.shape[1] // 768):
                cols = slice(t * 768, (t + 1) * 768)
                target[n, :, cols] = dot(piece, right[:, cols], TN).astype(BF16)


def dense_grads(saved):
    seqs = len(saved)
    width, hidden = saved[0][0].shape[1], saved[0][3].shape[1]
    return pl.pallas_call(
        functools.partial(dense_grads_kernel, seqs),
        out_shape=[
            jax.ShapeDtypeStruct((4, width // 4, width), BF16),
            jax.ShapeDtypeStruct((4, width // 4, hidden), BF16),
            jax.ShapeDtypeStruct((4, hidden // 4, width), BF16),
        ],
        in_specs=[VMEM] * (6 * seqs),
        out_specs=[VMEM] * 3,
        compiler_params=ROOM,
        cost_estimate=cost(10),
        name="dense_grads",
    )(*[member for group in saved for member in group])


def project_grads_kernel(seqs, sc, tok, *refs):
    fgs, refs = refs[:seqs], refs[seqs:]
    grads_in, refs = refs[: 2 * seqs], refs[2 * seqs :]
    wq, wk, wv, first, second, tg, grads, sums, full, sems = refs
    rows, width = tok.shape[1:]
    per = width // GROUPS
    heads = per // DH
    quarter = wq.shape[0] // 2
    copies = []
    for i, own in enumerate((wq, wk, wv)):
        part = pl.ds(i * quarter, quarter)
        copies += weight_copies(full.at[i], own, first.at[part], second.at[part], sems, 3 * i)
    for copy in copies:
        copy.start()

    def head(i, s, g, h):
        if i == 0:
            return grads_in[s][g, :, h * DH : (h + 1) * DH]
        start = h * 128 + (i - 1) * DH
        return grads_in[seqs + s][g, :, start : start + DH]

    def whole(i):
        each = [
            jnp.concatenate([head(i, s, g, h) for g in range(GROUPS) for h in range(heads)], 1)
            for s in range(seqs)
        ]
        return jnp.concatenate(each, 0)

    valid = jnp.concatenate([valid_rows(sc, s, rows) for s in range(seqs)], 0) > 0.0
    dq = whole(0)
    halves = [jnp.where(valid, whole(i), jnp.zeros((), BF16)) for i in (1, 2)]
    flat = tok[...].reshape(seqs * rows, width)
    for copy in copies:
        copy.wait()
    total = jnp.concatenate([fgs[s][...] for s in range(seqs)], 0)
    for i, grad in enumerate((dq, *halves)):
        total += dot(grad, full[i], NT)
        found = dot(flat, grad, TN).astype(BF16)
        half = width // 2
        for n in range(2):
            for t in range(width // 128):
                grads[t % 3, t // 3, n, i * half : (i + 1) * half, :] = found[
                    n * half : (n + 1) * half, t * 128 : (t + 1) * 128
                ]
    tg[...] = total.reshape(seqs, rows, width)
    sums[0:1, :] = jnp.sum(dq.astype(F32), 0, keepdims=True)
    sums[1:2, :] = jnp.sum(halves[1].astype(F32), 0, keepdims=True)
    sums[2:8, :] = jnp.zeros((6, width), F32)


def project_grads(sc, tok, fgs, grads, wq, wk, wv, first, second):
    seqs, rows, width = tok.shape
    return pl.pallas_call(
        functools.partial(project_grads_kernel, seqs),
        out_shape=[
            jax.ShapeDtypeStruct(tok.shape, F32),
            jax.ShapeDtypeStruct((3, 2, 2, 3 * (width // 2), 128), BF16),
            jax.ShapeDtypeStruct((8, width), F32),
        ],
        in_specs=[SMEM] + [VMEM] * (1 + len(fgs) + len(grads)) + [ANY] * 5,
        out_specs=[VMEM] * 3,
        scratch_shapes=[pltpu.VMEM((3, width, width), BF16), pltpu.SemaphoreType.DMA((9,))],
        compiler_params=ROOM,
        cost_estimate=cost(10),
        name="project_grads",
    )(sc, tok, *fgs, *grads, wq, wk, wv, first, second)


MESH = pl.DeviceIdType.MESH


def position():
    ctx = lax.axis_index("ctx")
    return ctx // 4, lax.rem(ctx // 2, 2), lax.rem(ctx, 2), lax.axis_index("wa")


def device(z, y, c, x):
    return z * 4 + y * 2 + c, x


def greet(others):
    barrier = pltpu.get_barrier_semaphore()
    for other in others:
        pl.semaphore_signal(barrier, inc=1, device_id=other, device_id_type=MESH)
    pl.semaphore_wait(barrier, len(others))


def send(src, dst, sems, to):
    copy = pltpu.make_async_remote_copy(
        src_ref=src,
        dst_ref=dst,
        send_sem=sems[0],
        recv_sem=sems[1],
        device_id=to,
        device_id_type=MESH,
    )
    copy.start()
    return copy


def add_low(left, right):
    return (left.astype(F32) + right.astype(F32)).astype(BF16)


def back_kernel(seqs, *refs):
    per_seq = 5
    ins = [refs[per_seq * s : per_seq * (s + 1)] for s in range(seqs)]
    a_own, a_give, b_own, b_give, rq, rkv, dense_out, *refs = refs[per_seq * seqs :]
    q_v, do_v, o_v, lse_v, kv_v, both, dkv, dq, delta, obuf, qbuf = refs[:11]
    from_core, from_y, a_v, b_v, a_in, b_in, a2, b2, a2_in, b2_in = refs[11:21]
    az_in, bz_in, dres, in_sem, c_sem, y_sem, z_sem, q_sem, l_sem, x_sem, dz_sem = refs[21:]
    z, y, c, x = position()
    sibling, beside, over = device(z, y, 1 - c, x), device(z, 1 - y, c, x), device(z, y, c, 1 - x)
    line = [None] + [device(z ^ d, y, c, x) for d in range(1, GROUPS)]
    greet([sibling, beside, over] + line[1:])

    def pair(sems, *index):
        return sems.at[(0, *index)], sems.at[(1, *index)]

    flow = {}
    flow["a"] = send(a_give, a_in, pair(x_sem, 0), over)
    flow["b"] = send(b_give, b_in, pair(x_sem, 1), beside)
    loads = []
    for s in range(seqs):
        targets = [ref.at[s] for ref in (q_v, do_v, o_v, lse_v, kv_v)]
        group = [
            pltpu.make_async_copy(src, dst, in_sem.at[s, i])
            for i, (src, dst) in enumerate(zip(ins[s], targets))
        ]
        for copy in group:
            copy.start()
        loads.append(group)
    own_loads = [
        pltpu.make_async_copy(a_own, a_v, l_sem.at[0]),
        pltpu.make_async_copy(b_own, b_v, l_sem.at[1]),
    ]
    for copy in own_loads:
        copy.start()

    rows = q_v.shape[1]
    heads = q_v.shape[2] // DH
    keys = kv_v.shape[1]
    tile, ktile = rows // 2, 2048
    quarter = keys // 4
    chunk = quarter // GROUPS
    ones = jnp.ones((8, DH), BF16)
    level = jnp.where(lax.broadcasted_iota(jnp.int32, (1, 128), 1) < DH, LN2, 1.0)
    waits = []

    def group_rows(g):
        return pl.ds(pl.multiple_of(g * chunk, chunk), chunk)

    def core_stage(u):
        flow["c", u] = send(
            obuf.at[u, pl.ds(2 * quarter, 2 * quarter)], from_core.at[u], pair(c_sem, u), sibling
        )

    def y_stage(u):
        flow["c", u].wait()
        second = pl.ds(quarter, quarter)
        obuf[u, second] = add_low(obuf[u, second], from_core[u, second])
        flow["y", u] = send(obuf.at[u, second], from_y.at[u], pair(y_sem, u), beside)
        obuf[u, 0:quarter] = add_low(obuf[u, 0:quarter], from_core[u, 0:quarter])

    def z_stage(u):
        flow["y", u].wait()
        obuf[u, 0:quarter] = add_low(obuf[u, 0:quarter], from_y[u])
        for d in range(1, GROUPS):
            src = obuf.at[u, group_rows(z ^ d)]
            waits.append(send(src, rkv.at[u, z], pair(z_sem, u, d), line[d]))
        own = pltpu.make_async_copy(obuf.at[u, group_rows(z)], rkv.at[u, z], z_sem.at[0, u, 0])
        own.start()
        waits.append(own)

    def q_stage(h):
        for d in range(1, GROUPS):
            waits.append(send(qbuf.at[h, z ^ d], rq.at[h, z], pair(q_sem, h, d), line[d]))
        own = pltpu.make_async_copy(qbuf.at[h, z], rq.at[h, z], q_sem.at[0, h, 0])
        own.start()
        waits.append(own)

    a_half, b_half = a2.shape[1], b2.shape[1]

    def dense_second():
        for copy in own_loads:
            copy.wait()
        flow["a"].wait()
        for slot, which in ((0, y), (1, 1 - y)):
            part = pl.ds(pl.multiple_of(which * a_half, 16), a_half)
            a2[slot] = add_low(a_v[part, :], a_in[part, :])
        flow["a"] = send(a2.at[1], a2_in, pair(x_sem, 2), beside)
        flow["b"].wait()
        for slot, which in ((0, x), (1, 1 - x)):
            b2[slot] = add_low(b_v[which], b_in[which])
        flow["b"] = send(b2.at[1], b2_in, pair(x_sem, 3), over)

    low_bit, high_bit = lax.rem(z, 2), z // 2
    parts = (("a", a2, a2_in, az_in), ("b", b2, b2_in, bz_in))

    def rows_at(start, n):
        return pl.ds(pl.multiple_of(start, 16), n)

    def dense_third():
        for i, (name, held, arrived, landing) in enumerate(parts):
            flow[name].wait()
            held[0] = add_low(held[0], arrived[...])
            n = held.shape[1] // 2
            src = held.at[0, rows_at((1 - low_bit) * n, n)]
            flow[name] = send(src, landing.at[0:n], pair(dz_sem, i, 0), line[1])

    def dense_fourth():
        for i, (name, held, _, landing) in enumerate(parts):
            flow[name].wait()
            n = held.shape[1] // 2
            mine = rows_at(low_bit * n, n)
            held[0, mine] = add_low(held[0, mine], landing[0:n])
            src = held.at[0, rows_at(low_bit * n + (1 - high_bit) * (n // 2), n // 2)]
            flow[name] = send(src, landing.at[n : n + n // 2], pair(dz_sem, i, 1), line[2])

    def dense_fifth():
        base = 0
        for name, held, _, landing in parts:
            flow[name].wait()
            n = held.shape[1] // 2
            mine = rows_at(low_bit * n + high_bit * (n // 2), n // 2)
            dres[base : base + n // 2] = add_low(held[0, mine], landing[n : n + n // 2])
            base += n // 2

    units = [(h, s) for h in range(heads) for s in range(seqs)]
    slots = {}
    for u in range(len(units) - 1):
        slots.setdefault(2 * u + 3, []).append(functools.partial(y_stage, u))
        slots.setdefault(2 * u + 5, []).append(functools.partial(z_stage, u))
    slots.setdefault(5, []).append(dense_second)
    slots.setdefault(7, []).append(dense_third)
    slots.setdefault(9, []).append(dense_fourth)
    slots.setdefault(12, []).append(dense_fifth)

    for u, (h, s) in enumerate(units):
        hs = slice(h * DH, (h + 1) * DH)
        lanes = slice(h * 128, (h + 1) * 128)
        if h == 0:
            for copy in loads[s]:
                copy.wait()
        for n in range(2):
            for work in slots.get(2 * u + n, []):
                work()
            part = slice(n * tile, (n + 1) * tile)
            q, do, o = q_v[s, part, hs], do_v[s, part, hs], o_v[s, part, hs]
            zero = jnp.zeros_like(q)
            both[0:tile, :] = jnp.concatenate([q, zero], 1)
            both[tile : 2 * tile, :] = jnp.concatenate([zero, do], 1)
            product = do.astype(F32) * o.astype(F32)
            high = product.astype(BF16)
            remains = (product - high.astype(F32)).astype(BF16)
            delta[...] = dot(ones, high, NT) + dot(ones, remains, NT)
            dq[...] = jnp.zeros_like(dq)

            def step(j, _, u=u, s=s, h=h, n=n, part=part, lanes=lanes):
                span = pl.ds(pl.multiple_of(j * ktile, ktile), ktile)
                kv = kv_v[s, span, lanes]
                b = both[...]
                found = dot(kv, b, NT)
                p = jnp.exp2(jnp.minimum(found[:, :tile] - lse_v[s, h, 0:1, part], 1.0))
                ds = (p * (found[:, tile:] - delta[0:1, :])).astype(BF16)
                grads = dot(jnp.concatenate([ds, p.astype(BF16)], 1), b)
                if n == 0:
                    dkv[span, :] = grads
                else:
                    obuf[u, span, :] = ((dkv[span, :] + grads) * level).astype(BF16)
                dq[...] += dot(ds, kv, TN)
                return 0

            lax.fori_loop(0, keys // ktile, step, 0)
            found = (dq[:, :DH] * DH**-0.5).astype(BF16)
            for i in range(2):
                qbuf[h, 2 * n + i, :, s * DH : (s + 1) * DH] = found[
                    i * (tile // 2) : (i + 1) * (tile // 2)
                ]
        core_stage(u)
        if s == seqs - 1:
            q_stage(h)
    last = len(units) - 1
    for n in sorted(n for n in slots if n >= 2 * len(units)):
        for work in slots[n]:
            work()
    y_stage(last)
    z_stage(last)
    for copy in waits:
        copy.wait()
    done = pltpu.make_async_copy(dres, dense_out, l_sem.at[0])
    done.start()
    done.wait()


def attend_back_all(seqs_in, ready):
    seqs = len(seqs_in)
    q, _, _, lse, held = seqs_in[0]
    rows, per = q.shape
    heads = per // DH
    units = heads * seqs
    keys = held.shape[0]
    chunk = rows // GROUPS
    a, b = ready[0].shape, ready[2].shape
    a_half, b_half, half = a[0] // 2, b[1], a[1]
    dma = pltpu.SemaphoreType.DMA
    return pl.pallas_call(
        functools.partial(back_kernel, seqs),
        out_shape=[
            jax.ShapeDtypeStruct((heads, GROUPS, chunk, 128), BF16),
            jax.ShapeDtypeStruct((units, GROUPS, chunk, 128), BF16),
            jax.ShapeDtypeStruct(((a_half + b_half) // 4, half), BF16),
        ],
        in_specs=[ANY] * (5 * seqs + 4),
        out_specs=[ANY] * 3,
        scratch_shapes=[
            pltpu.VMEM((seqs, rows, per), BF16),
            pltpu.VMEM((seqs, rows, per), BF16),
            pltpu.VMEM((seqs, rows, per), BF16),
            pltpu.VMEM((seqs, *lse.shape), F32),
            pltpu.VMEM((seqs, keys, 2 * per), BF16),
            pltpu.VMEM((rows, 128), BF16),
            pltpu.VMEM((keys, 128), F32),
            pltpu.VMEM((rows // 2, 128), F32),
            pltpu.VMEM((8, rows // 2), F32),
            pltpu.VMEM((units, keys, 128), BF16),
            pltpu.VMEM((heads, GROUPS, chunk, 128), BF16),
            pltpu.VMEM((units, keys // 2, 128), BF16),
            pltpu.VMEM((units, keys // 4, 128), BF16),
            pltpu.VMEM(a, BF16),
            pltpu.VMEM(b, BF16),
            pltpu.VMEM(a, BF16),
            pltpu.VMEM(b, BF16),
            pltpu.VMEM((2, a_half, half), BF16),
            pltpu.VMEM((2, b_half, half), BF16),
            pltpu.VMEM((a_half, half), BF16),
            pltpu.VMEM((b_half, half), BF16),
            pltpu.VMEM((3 * a_half // 4, half), BF16),
            pltpu.VMEM((3 * b_half // 4, half), BF16),
            pltpu.VMEM(((a_half + b_half) // 4, half), BF16),
            dma((seqs, 5)),
            dma((2, units)),
            dma((2, units)),
            dma((2, units, GROUPS)),
            dma((2, heads, GROUPS)),
            dma((2,)),
            dma((2, 4)),
            dma((2, 2, 2)),
        ],
        compiler_params=pltpu.CompilerParams(
            vmem_limit_bytes=63 * 2**20, collective_id=1, has_side_effects=True
        ),
        cost_estimate=cost(120),
        name="attend_back_all",
    )(*[member for group in seqs_in for member in group], *ready)


def vector_of(vec, row, half):
    both = [vec[k, row + 1 : row + 2, :half].astype(F32) for k in range(2)]
    return jnp.concatenate(both, 1)


def start_kernel(seqs, lengths, order, tokens, wq, wk, wv, wo, wi, wu, *refs):
    sc = Counts(lengths, order)
    vectors, refs = refs[:9], refs[9:]
    q_out, kv_out, o_out, lse_out = (refs[i * seqs : (i + 1) * seqs] for i in range(4))
    refs = refs[4 * seqs :]
    back_out, vec_out, others, *dense_out = refs[:6]
    full, q_held, kv_held, vec, own_vec, tok, *refs = refs[6:]
    q_v, kv_v, o_v, lse_v, shade, qa, acc, sums, top, *sems = refs
    v_sem, wx_sem, wy_sem, wc_sem, l_sem, dx_sem, dc_sem, q_sem, z_sem, y_sem, c_sem = sems[:11]
    own_sem, b_sem = sems[11:]
    z, y, c, x = position()
    sibling, beside, over = device(z, y, 1 - c, x), device(z, 1 - y, c, x), device(z, y, c, 1 - x)
    line = [None] + [device(z ^ d, y, c, x) for d in range(1, GROUPS)]
    greet([sibling, beside, over] + line[1:])

    def pair(sem, *index):
        return sem.at[(0, *index)], sem.at[(1, *index)]

    waits = []
    half = wq.shape[0]
    eighth = half // 4

    def rows_of(which, cc, yy):
        start = which * half + (2 * cc + yy) * eighth
        return pl.ds(pl.multiple_of(start, 16), eighth)

    own_rows = pl.ds(pl.multiple_of((2 * c + y) * eighth, 16), eighth)
    tok_in = pltpu.make_async_copy(tokens, tok, l_sem.at[6])
    tok_in.start()
    flow = {}
    turns = (1, 2, 0)
    locals_of = []
    for i in turns:
        own = (wq, wk, wv)[i]
        flow["x", i] = send(
            own.at[own_rows], full.at[i, rows_of(x, c, y)], pair(wx_sem, i), over
        )
    for i in turns:
        own = (wq, wk, wv)[i]
        place = full.at[i, pl.ds(pl.multiple_of(x * half, half), half)]
        copy = pltpu.make_async_copy(own, place, l_sem.at[i])
        copy.start()
        locals_of.append(copy)
    own_vec[...] = jnp.zeros_like(own_vec)
    for i, one in enumerate(vectors):
        row = (i + 1) % len(vectors)
        own_vec[row : row + 1, : one.shape[0]] = one[...].astype(F32)[None].astype(BF16)
    vec[x] = own_vec[...]
    vec_flow = send(own_vec, vec.at[x], pair(v_sem), over)

    def after_x(i):
        flow["x", i].wait()
        got = full.at[i, rows_of(1 - x, c, y)]
        flow["y", i] = send(got, got, pair(wy_sem, i), beside)
        flow["c", i, 0] = send(got, got, pair(wc_sem, i, 0), sibling)

    def after_y(i):
        flow["y", i].wait()
        got = full.at[i, rows_of(1 - x, c, 1 - y)]
        flow["c", i, 1] = send(got, got, pair(wc_sem, i, 1), sibling)

    def after_core(i):
        flow["c", i, 0].wait()
        flow["c", i, 1].wait()

    rows, width = tok.shape[1:]
    per = width // GROUPS
    heads = per // DH
    tok_in.wait()
    flat = tok[...].reshape(seqs * rows, width)
    valid = jnp.concatenate([valid_rows(sc, s, rows) for s in range(seqs)], 0) > 0.0
    lane = lax.broadcasted_iota(jnp.int32, (8, BLK), 1)
    for piece, offset in enumerate((0, 2, 1, 3)):
        owner = lax.bitwise_xor(2 * y + c, offset)
        for g in range(GROUPS):
            for k in range(2):
                start_of = order[(4 * g + owner) * 2 + k] * BLK
                for s in range(seqs):
                    inside = lane + start_of < lengths[s]
                    cols = slice((2 * g + k) * BLK, (2 * g + k + 1) * BLK)
                    shade[s, piece, :, cols] = jnp.where(inside, 0.0, -1e30)
    after_x(1)
    after_x(2)
    after_y(1)
    after_x(0)
    dense_weights = (wo, wi, wu)
    for i, weight in enumerate(dense_weights):
        n = weight.shape[0] // 2
        part = pl.ds(pl.multiple_of(c * n, 16), n)
        flow["dx", i] = send(weight.at[part], dense_out[i].at[part], pair(dx_sem, i), over)
    after_y(2)
    vec_flow.wait()

    def bias(row):
        return vector_of(vec, row, half)

    for copy in locals_of:
        copy.wait()
    after_core(1)
    keys = jnp.where(valid, dot(flat, full[1]), 0.0).astype(BF16)
    after_y(0)
    after_core(2)
    values = jnp.where(valid, dot(flat, full[2]) + bias(1), 0.0).astype(BF16)
    for s in range(seqs):
        rs = slice(s * rows, (s + 1) * rows)
        for g in range(GROUPS):
            for h in range(heads):
                cols = slice(g * per + h * DH, g * per + (h + 1) * DH)
                kv_held[s, g, :, h * 128 : (h + 1) * 128] = jnp.concatenate(
                    [keys[rs, cols], values[rs, cols]], 1
                )

    def kv_sends(s):
        for d in range(1, GROUPS):
            flow["z", s, d] = send(
                kv_held.at[s, z ^ d], kv_v.at[s, 0, z], pair(z_sem, s, d), line[d]
            )

    def q_sends(s):
        for d in range(1, GROUPS):
            flow["q", s, d] = send(q_held.at[s, z ^ d], q_v.at[s, z], pair(q_sem, s, d), line[d])

    kv_sends(0)

    def pass_on(s, d, src):
        g = z ^ d
        flow["ky", s, d] = send(src, kv_v.at[s, 1, g], pair(y_sem, s, d), beside)
        flow["kc", s, d, 0] = send(src, kv_v.at[s, 2, g], pair(c_sem, s, d, 0), sibling)

    def pass_core(s, d):
        flow["ky", s, d].wait()
        got = kv_v.at[s, 1, z ^ d]
        flow["kc", s, d, 1] = send(got, kv_v.at[s, 3, z ^ d], pair(c_sem, s, d, 1), sibling)

    pass_on(0, 0, kv_held.at[0, z])
    after_core(0)
    queries = ((dot(flat, full[0]) + bias(0)) * (DH**-0.5 / LN2)).astype(BF16)
    for s in range(seqs):
        rs = slice(s * rows, (s + 1) * rows)
        for g in range(GROUPS):
            q_held[s, g] = queries[rs, g * per : (g + 1) * per]
    for i in range(3):
        place = full.at[i, pl.ds(pl.multiple_of((1 - x) * half, half), half)]
        copy = pltpu.make_async_copy(place, others.at[i], l_sem.at[3 + i])
        copy.start()
        waits.append(copy)
    copy = pltpu.make_async_copy(vec, vec_out, l_sem.at[7])
    copy.start()
    waits.append(copy)
    q_sends(0)
    for s in range(seqs):
        kv_v[s, 0, z] = kv_held[s, z]
        q_v[s, z] = q_held[s, z]

    def arrive(s, d):
        flow["z", s, d].wait()
        pass_on(s, d, kv_v.at[s, 0, z ^ d])

    def own_and_core(s):
        for d in range(GROUPS):
            flow["kc", s, d, 0].wait()

    def dense_core(i):
        flow["dx", i].wait()
        n = dense_weights[i].shape[0] // 2
        got = dense_out[i].at[pl.ds(pl.multiple_of(c * n, 16), n)]
        waits.append(send(got, got, pair(dc_sem, i), sibling))

    def leave(src, dst, i):
        copy = pltpu.make_async_copy(src, dst, b_sem.at[i])
        copy.start()
        waits.append(copy)

    def attend_part(s, h, pieces):
        lanes = slice(h * 128, (h + 1) * 128)
        count, tile = GROUPS * rows, 256

        def step(j, _):
            piece = pieces[0] + j * (pieces[1] - pieces[0])
            kv = kv_v[s, piece, :, :, lanes].reshape(count, 128)
            dark = shade[s, piece, 0:1, :]
            for n in range(count // tile):
                part = slice(n * tile, (n + 1) * tile)
                scores = dot(qa[part, :], kv, NT) + dark
                high = scores[:, :128]
                for i in range(1, count // 128):
                    high = jnp.maximum(high, scores[:, i * 128 : (i + 1) * 128])
                old = top[part, :]
                new = jnp.maximum(old, jnp.max(high, 1, keepdims=True))
                fade = jnp.exp2(old - new)
                each = [
                    jnp.exp2(scores[:, i * 128 : (i + 1) * 128] - new) for i in range(count // 128)
                ]
                sums[part, :] = sums[part, :] * fade + sum(each)
                p = jnp.concatenate([one.astype(BF16) for one in each], 1)
                acc[part, :] = acc[part, :] * fade + dot(p, kv)
                top[part, :] = new
            return 0

        lax.fori_loop(0, 2, step, 0)

    def attend_begin(s, h):
        hs = slice(h * DH, (h + 1) * DH)
        mine = q_v[s, :, :, hs].reshape(GROUPS * rows, DH)
        qa[...] = jnp.concatenate([mine, jnp.zeros_like(mine)], 1)
        acc[...] = jnp.zeros_like(acc)
        sums[...] = jnp.zeros_like(sums)
        top[...] = jnp.full_like(top, -1e30)

    def attend_end(s, h):
        hs = slice(h * DH, (h + 1) * DH)
        total = jnp.sum(sums[...], 1, keepdims=True)
        logs = top[...] + jnp.log2(jnp.broadcast_to(total, top.shape))
        lse_v[s, h] = jnp.transpose(logs)[:8]
        found = (acc[:, DH:] * (1.0 / total)).astype(BF16)
        o_v[s, :, :, hs] = found.reshape(GROUPS, rows, DH)

    for d in range(1, GROUPS):
        arrive(0, d)
        if d > 1:
            pass_core(0, d - 2)
    kv_sends(1)
    pass_on(1, 0, kv_held.at[1, z])
    pass_core(0, 2)
    pass_core(0, 3)
    for d in range(1, GROUPS):
        flow["q", 0, d].wait()
    q_sends(1)
    own_and_core(0)
    slots = {
        2: (lambda: pass_core(1, 0), lambda: arrive(1, 1)),
        3: (lambda: arrive(1, 2), lambda: arrive(1, 3)),
        4: (lambda: pass_core(1, 1), lambda: dense_core(0)),
        5: (lambda: pass_core(1, 2),),
        6: (lambda: own_and_core(1), lambda: [flow["q", 1, d].wait() for d in range(1, GROUPS)]),
        7: (lambda: pass_core(1, 3),),
        8: (lambda: dense_core(1),),
        10: (lambda: dense_core(2),),
    }
    for s in range(seqs):
        for h in range(heads):
            for n, pieces in enumerate(((0, 2), (1, 3))):
                for work in slots.get(6 * s + 2 * h + n, ()):
                    work()
                if n == 0:
                    attend_begin(s, h)
                if h == 0 and n == 1:
                    for d in range(GROUPS):
                        flow["kc", s, d, 1].wait()
                attend_part(s, h, pieces)
            attend_end(s, h)
        if s == 0:
            for d in range(1, GROUPS):
                waits.append(
                    send(o_v.at[0, z ^ d], back_out.at[z], pair(own_sem, d), line[d])
                )
            leave(o_v.at[0, z], back_out.at[z], 4 * seqs)
        for i, (src, dst) in enumerate(
            ((q_v, q_out), (kv_v, kv_out), (o_v, o_out), (lse_v, lse_out))
        ):
            leave(src.at[s], dst[s], 4 * s + i)
    for copy in waits:
        copy.wait()


def start(lengths, order, tok, weights, vectors):
    seqs, rows, width = tok.shape
    per = width // GROUPS
    half = weights[0].shape[0]
    joined = (16, vectors[-1].shape[0])
    heads, total = per // DH, GROUPS * rows
    narrow = jax.ShapeDtypeStruct((GROUPS, rows, per), BF16)
    dma = pltpu.SemaphoreType.DMA
    return pl.pallas_call(
        functools.partial(start_kernel, seqs),
        out_shape=[narrow] * seqs
        + [jax.ShapeDtypeStruct((4, GROUPS, rows, 2 * per), BF16)] * seqs
        + [narrow] * seqs
        + [jax.ShapeDtypeStruct((heads, 8, total), F32)] * seqs
        + [
            narrow,
            jax.ShapeDtypeStruct((2, *joined), BF16),
            jax.ShapeDtypeStruct((3, half, width), BF16),
        ]
        + [jax.ShapeDtypeStruct(w.shape, BF16) for w in weights[3:]],
        in_specs=[SMEM] * 2 + [ANY] * 7 + [VMEM] * 9,
        out_specs=[ANY] * (4 * seqs + 6),
        scratch_shapes=[
            pltpu.VMEM((3, width, width), BF16),
            pltpu.VMEM((seqs, GROUPS, rows, per), BF16),
            pltpu.VMEM((seqs, GROUPS, rows, 2 * per), BF16),
            pltpu.VMEM((2, *joined), BF16),
            pltpu.VMEM(joined, BF16),
            pltpu.VMEM(tok.shape, BF16),
            pltpu.VMEM((seqs, GROUPS, rows, per), BF16),
            pltpu.VMEM((seqs, 4, GROUPS, rows, 2 * per), BF16),
            pltpu.VMEM((seqs, GROUPS, rows, per), BF16),
            pltpu.VMEM((seqs, heads, 8, total), F32),
            pltpu.VMEM((seqs, 4, 8, total), F32),
            pltpu.VMEM((total, 128), BF16),
            pltpu.VMEM((total, 128), F32),
            pltpu.VMEM((total, 128), F32),
            pltpu.VMEM((total, 128), F32),
            dma((2,)),
            dma((2, 3)),
            dma((2, 3)),
            dma((2, 3, 2)),
            dma((8,)),
            dma((2, 3)),
            dma((2, 3)),
            dma((2, seqs, GROUPS)),
            dma((2, seqs, GROUPS)),
            dma((2, seqs, GROUPS)),
            dma((2, seqs, GROUPS, 2)),
            dma((2, GROUPS)),
            dma((4 * seqs + 1,)),
        ],
        compiler_params=pltpu.CompilerParams(
            vmem_limit_bytes=63 * 2**20, collective_id=4, has_side_effects=True
        ),
        cost_estimate=cost(80),
        name="start",
    )(lengths, order, tok, *weights, *vectors)


def middle_stage(s, att, mask, tok, teach, vec, weights, keep, outs, first_done, outer_done):
    wo, wi, wu, slope = weights
    att_k, br_k, hl_k, il_k, act_k, ol_k = keep
    out, fg, sums, wide_sums = outs
    rows = att.shape[0]
    hidden = wi.shape[1]
    tile = 512
    rs = slice(s * rows, (s + 1) * rows)
    half = tok.shape[2] // 2
    out_bias, gain_one, shift_one, outer_bias, gain_two, shift_two = (
        vector_of(vec, row, half) for row in range(2, 8)
    )
    add = functools.partial(jnp.sum, axis=0, keepdims=True)

    def collect(target, value):
        if s == 0:
            target[...] = value
        else:
            target[...] += value

    att_k[rs, :] = att
    first_done[0]()
    first = tok[s].astype(F32) + dot(att, wo[...]) + out_bias
    normed_one, inverse_one = norm(first)
    hidden_in = normed_one * gain_one + shift_one
    hl = hidden_in.astype(BF16)
    hl_k[rs, :] = hl
    first_done[1]()
    second = hidden_in + outer_bias
    for n in range(hidden // tile):
        cols = slice(n * tile, (n + 1) * tile)
        k, begin = divmod(n * tile, hidden // 2)
        inner = dot(hl, wi[:, cols]) + vec[k, 0:1, begin : begin + tile].astype(F32)
        below, density = normal_parts(inner)
        act = (inner * below).astype(BF16)
        act_k[rs, cols] = act
        slope[:, cols] = below + inner * density
        second += dot(act, wu[cols, :])
    normed_two, inverse_two = norm(second)
    final = normed_two * gain_two + shift_two
    out[s] = final.astype(BF16)
    residue = (final - teach[s].astype(F32)) * mask
    collect(sums.at[0:1], add(residue * normed_two))
    collect(sums.at[1:2], add(residue))
    collect(sums.at[6:7], add(residue * residue))
    second_grad = norm_back(residue * gain_two, normed_two, inverse_two)
    ol = second_grad.astype(BF16)
    ol_k[rs, :] = ol
    collect(sums.at[2:3], add(ol.astype(F32)))
    outer_done()
    hidden_grad = second_grad
    for n in range(hidden // tile):
        cols = slice(n * tile, (n + 1) * tile)
        il = (dot(ol, wu[cols, :], NT) * slope[:, cols]).astype(BF16)
        il_k[rs, cols] = il
        collect(wide_sums.at[0:1, cols], add(il.astype(F32)))
        hidden_grad += dot(il, wi[:, cols], NT)
    first_grad = norm_back(hidden_grad * gain_one, normed_one, inverse_one)
    fg[s] = first_grad
    br = first_grad.astype(BF16)
    br_k[rs, :] = br
    collect(sums.at[3:4], add(hidden_grad * normed_one))
    collect(sums.at[4:5], add(hidden_grad))
    collect(sums.at[5:6], add(br.astype(F32)))
    return dot(br, wo[...], NT).astype(BF16)


def middle_kernel(seqs, lengths, order, tok, teach, vec, *refs):
    sc = Counts(lengths, order)
    attended, weights, refs = refs[:seqs], refs[seqs : seqs + 6], refs[seqs + 6 :]
    out, fg, sums, wide_sums, a_own, a_give, b_own, b_give = refs[:8]
    grads_in, refs = refs[8 : 8 + seqs], refs[8 + seqs :]
    wo, wi, wu, slope, o_in, g_out, att_k, br_k, hl_k, il_k, act_k, ol_k = refs[:12]
    own, given, w_sem, o_sem, g_sem, c_sem = refs[12:]
    z, y, c, x = position()
    sibling = device(z, y, 1 - c, x)
    line = [None] + [device(z ^ d, y, c, x) for d in range(1, GROUPS)]
    greet([sibling] + line[1:])
    coming, going = {}, {}
    for s in range(seqs):
        if s == 0:
            coming[s, 0] = pltpu.make_async_copy(attended[s], o_in.at[s], o_sem.at[0, s, 0])
            coming[s, 0].start()
            continue
        for d in range(1, GROUPS):
            sems = o_sem.at[0, s, d], o_sem.at[1, s, d]
            coming[s, d] = send(attended[s].at[z ^ d], o_in.at[s, z], sems, line[d])
        coming[s, 0] = pltpu.make_async_copy(attended[s].at[z], o_in.at[s, z], o_sem.at[0, s, 0])
        coming[s, 0].start()
    copies = [
        half_copies(full, *weights[2 * i : 2 * i + 2], w_sem, 2 * i)
        for i, full in enumerate((wo, wi, wu))
    ]
    for group in copies:
        for copy in group:
            copy.start()

    def loaded(which):
        for i in which:
            for copy in copies[i]:
                copy.wait()

    half = wo.shape[0] // 2
    blocks = wi.shape[1] // (2 * half)
    base = (1 + blocks) * half
    core = []

    def store(k, start, value):
        low_value = value.astype(BF16)
        own[0, k, start : start + half, :] = low_value[:, :half]
        own[1, k, start : start + half, :] = low_value[:, half:]

    def pass_core(k, start, stop):
        place = pl.ds(start, stop - start)
        i = len(core)
        sems = c_sem.at[0, i], c_sem.at[1, i]
        core.append(send(own.at[1 - c, k, place], given.at[k, place], sems, sibling))

    def outer_grads():
        for k in range(2):
            for t in range(blocks):
                rows_of = slice((k * blocks + t) * half, (k * blocks + t + 1) * half)
                store(k, base + t * half, dot(act_k[:, rows_of], ol_k[...], TN))
            pass_core(k, base, base + blocks * half)

    rows = tok.shape[1]
    per = o_in.shape[3]
    for s in range(seqs):
        for d in range(GROUPS if s > 0 else 1):
            coming[s, d].wait()
        att = jnp.concatenate([o_in[s, g] for g in range(GROUPS)], 1)
        mask = valid_rows(sc, s, rows)
        waits = (lambda: loaded([0]), lambda: loaded([1, 2])) if s == 0 else (lambda: None,) * 2
        found = middle_stage(
            s,
            att,
            mask,
            tok,
            teach,
            vec,
            (wo, wi, wu, slope),
            (att_k, br_k, hl_k, il_k, act_k, ol_k),
            (out, fg, sums, wide_sums),
            waits,
            outer_grads if s == seqs - 1 else lambda: None,
        )
        for g in range(GROUPS):
            g_out[s, g] = found[:, g * per : (g + 1) * per]
        for d in range(1, GROUPS):
            sems = g_sem.at[0, s, d], g_sem.at[1, s, d]
            going[s, d] = send(g_out.at[s, z ^ d], grads_in[s].at[z], sems, line[d])
        going[s, 0] = pltpu.make_async_copy(g_out.at[s, z], grads_in[s].at[z], g_sem.at[0, s, 0])
        going[s, 0].start()
    sums[7:8, :] = jnp.zeros((1, sums.shape[1]), F32)

    for k in range(2):
        ks = slice(k * half, (k + 1) * half)
        store(k, 0, dot(att_k[:, ks], br_k[...], TN))
        for t in range(blocks):
            cols = slice(2 * t * half, 2 * (t + 1) * half)
            store(k, (1 + t) * half, dot(hl_k[:, ks], il_k[:, cols], TN))
        pass_core(k, 0, base)
    for copy in core:
        copy.wait()
    mine = own.at[c]
    cut, b_half = a_own.shape[0], b_own.shape[1]
    a_own[...] = add_low(mine[x, 0:cut], given[x, 0:cut])
    a_give[...] = add_low(mine[1 - x, 0:cut], given[1 - x, 0:cut])
    for k in range(2):
        for target, which in ((b_own, y), (b_give, 1 - y)):
            part = pl.ds(pl.multiple_of(cut + which * b_half, 16), b_half)
            target[k] = add_low(mine[k, part], given[k, part])
    for copy in going.values():
        copy.wait()


def cut_of(total):
    return total // 256 * 128


def middle(lengths, order, tok, teach, vec, attended, weights):
    seqs, rows, width = tok.shape
    hidden = 2 * vec.shape[2]
    half = width // 2
    total = half + hidden
    cut = cut_of(total)
    dma = pltpu.SemaphoreType.DMA
    narrow, wide = (seqs * rows, width), (seqs * rows, hidden)
    b_shape = jax.ShapeDtypeStruct((2, (total - cut) // 2, half), BF16)
    a_shape = jax.ShapeDtypeStruct((cut, half), BF16)
    groups, _, per = attended[0].shape
    return pl.pallas_call(
        functools.partial(middle_kernel, seqs),
        out_shape=[
            jax.ShapeDtypeStruct(tok.shape, BF16),
            jax.ShapeDtypeStruct(tok.shape, F32),
            jax.ShapeDtypeStruct((8, width), F32),
            jax.ShapeDtypeStruct((1, hidden), F32),
            a_shape,
            a_shape,
            b_shape,
            b_shape,
        ]
        + [jax.ShapeDtypeStruct(a.shape, BF16) for a in attended],
        in_specs=[SMEM] * 2 + [VMEM] * 3 + [ANY] * (seqs + 6),
        out_specs=[VMEM] * 8 + [ANY] * seqs,
        scratch_shapes=[
            pltpu.VMEM((width, width), BF16),
            pltpu.VMEM((width, hidden), BF16),
            pltpu.VMEM((hidden, width), BF16),
            pltpu.VMEM((rows, hidden), F32),
            pltpu.VMEM((seqs, groups, rows, per), BF16),
            pltpu.VMEM((seqs, groups, rows, per), BF16),
            pltpu.VMEM(narrow, BF16),
            pltpu.VMEM(narrow, BF16),
            pltpu.VMEM(narrow, BF16),
            pltpu.VMEM(wide, BF16),
            pltpu.VMEM(wide, BF16),
            pltpu.VMEM(narrow, BF16),
            pltpu.VMEM((2, 2, total, half), BF16),
            pltpu.VMEM((2, total, half), BF16),
            dma((6,)),
            dma((2, seqs, groups)),
            dma((2, seqs, groups)),
            dma((2, 4)),
        ],
        compiler_params=pltpu.CompilerParams(
            vmem_limit_bytes=63 * 2**20, collective_id=3, has_side_effects=True
        ),
        cost_estimate=cost(60),
        name="middle",
    )(lengths, order, tok, teach, vec, *attended, *weights)


def finish_kernel(
    seqs, lengths, order, tok, fg, rq, rkv, dense_sums, wide_sums, ready, wq, wk, wv, others, *rest
):
    sc = Counts(lengths, order)
    tg, out, dense_out, small_out, *rest = rest
    full, grads, acc, from_core, from_x, from_y, from_z, res, vec, vec_in, dense_res = rest[:11]
    w_sems, sems, small_sems, d_sems, last_sem = rest[11:]
    z, y, c, x = position()
    sibling, beside, over = device(z, y, 1 - c, x), device(z, 1 - y, c, x), device(z, y, c, 1 - x)
    line = [None] + [device(z ^ d, y, c, x) for d in range(1, GROUPS)]
    greet([sibling, beside, over] + line[1:])

    a_half = cut_of(dense_res.shape[1]) // 2
    b_half = dense_res.shape[1] // 2 - a_half
    low_bit, high_bit = lax.rem(z, 2), z // 2
    dense_parts = ((0, a_half, y * a_half), (a_half // 4, b_half, 2 * a_half + y * b_half))

    def dense_rows(start, n):
        return dense_res.at[c, pl.ds(pl.multiple_of(start, 16), n)]

    def d_pair(k, i):
        return d_sems.at[0, k, i], d_sems.at[1, k, i]

    dense_flows = []
    for i, (start, n, base) in enumerate(dense_parts):
        place = dense_rows(base + low_bit * (n // 2) + high_bit * (n // 4), n // 4)
        src = ready.at[start : start + n // 4]
        place[...] = src[...]
        dense_flows.append(send(src, place, d_pair(0, i), line[2]))

    def dense_near():
        for i, (_, n, base) in enumerate(dense_parts):
            dense_flows[i].wait()
            place = dense_rows(base + low_bit * (n // 2), n // 2)
            dense_flows[i] = send(place, place, d_pair(1, i), line[1])

    def dense_y():
        for i, (_, n, base) in enumerate(dense_parts):
            dense_flows[i].wait()
            place = dense_rows(base, n)
            dense_flows[i] = send(place, place, d_pair(2, i), beside)

    def dense_core():
        for i, (_, n, _) in enumerate(dense_parts):
            dense_flows[i].wait()
            place = dense_res.at[c, pl.ds(2 * a_half * i, 2 * n)]
            dense_flows[i] = send(place, place, d_pair(3, i), sibling)

    rows, width = tok.shape[1:]
    heads = width // GROUPS // DH
    copies = []
    for i, own in enumerate((wq, wk, wv)):
        copies += half_copies(full.at[i], own, others.at[i], w_sems, 2 * i)
    for copy in copies:
        copy.start()

    def head(i, s, g, h):
        if i == 0:
            return rq[h, g, :, s * DH : (s + 1) * DH]
        return rkv[h * seqs + s, g, :, (i - 1) * DH : i * DH]

    def whole(i):
        each = [
            jnp.concatenate([head(i, s, g, h) for g in range(GROUPS) for h in range(heads)], 1)
            for s in range(seqs)
        ]
        return jnp.concatenate(each, 0)

    valid = jnp.concatenate([valid_rows(sc, s, rows) for s in range(seqs)], 0) > 0.0
    parted = [whole(0)] + [jnp.where(valid, whole(i), jnp.zeros((), BF16)) for i in (1, 2)]
    flat = tok[...].reshape(seqs * rows, width)
    wide = width // 2
    for i, grad in enumerate(parted):
        found = dot(flat, grad, TN).astype(BF16)
        for n in range(2):
            for t in range(width // 128):
                grads[t % 3, t // 3, n, i * wide : (i + 1) * wide, :] = found[
                    n * wide : (n + 1) * wide, t * 128 : (t + 1) * 128
                ]
    lines_of = [dense_sums[i : i + 1, :] for i in range(7)]
    lines_of += [jnp.sum(grad.astype(F32), 0, keepdims=True) for grad in (parted[0], parted[2])]
    lines_of.append(wide_sums[...])
    row = 0
    for one in lines_of:
        for t in range(one.shape[1] // 128):
            vec[row : row + 1, :] = one[:, t * 128 : (t + 1) * 128]
            row += 1
    valid_count = sum(jnp.clip(sc[i], 0, BLK) for i in range(2 * seqs))
    vec[row:, :] = jnp.full((vec.shape[0] - row, 128), valid_count.astype(F32))

    parts, rows_each = grads.shape[0], grads.shape[3]
    half, piece = rows_each // 2, rows_each // 8
    own_half = pl.ds(pl.multiple_of(y * half, half), half)
    other_half = pl.ds(pl.multiple_of((1 - y) * half, half), half)

    def piece_of(g):
        return pl.ds(pl.multiple_of(y * half + g * piece, piece), piece)

    def pair(k, p):
        return sems.at[0, k, p], sems.at[1, k, p]

    def small_pair(k):
        return small_sems.at[0, k], small_sems.at[1, k]

    core = [
        send(grads.at[p, 1 - c], from_core.at[p], pair(0, p), sibling) for p in range(parts)
    ]
    short = send(vec, vec_in.at[0], small_pair(0), sibling)
    flows = []
    for p in range(parts):
        core[p].wait()
        acc[p] = add_low(grads[p, c], from_core[p])
        if p == 1:
            flows.append(send(acc.at[p, :, other_half], from_y.at[p], pair(1, p), beside))
        else:
            flows.append(send(acc.at[p, 1 - x], from_x.at[p], pair(1, p), over))
    dense_near()
    for copy in copies:
        copy.wait()
    total = jnp.concatenate([fg[s] for s in range(seqs)], 0)
    for i, grad in enumerate(parted):
        total += dot(grad, full[i], NT)
    tg[...] = total.reshape(seqs, rows, width)
    short.wait()
    vec_in[8] = vec[...] + vec_in[0]
    short = send(vec_in.at[8], vec_in.at[1], small_pair(1), over)
    for p in (1, 0, 2):
        flows[p].wait()
        if p == 1:
            for k in range(2):
                acc[p, k, own_half] = add_low(acc[p, k, own_half], from_y[p, k])
            flows[p] = send(acc.at[p, 1 - x, own_half], from_x.at[p, own_half], pair(2, p), over)
        else:
            acc[p, x] = add_low(acc[p, x], from_x[p])
            flows[p] = send(acc.at[p, x, other_half], from_y.at[p, 0], pair(2, p), beside)
    short.wait()
    vec[...] = vec_in[8] + vec_in[1]
    short = send(vec, vec_in.at[2], small_pair(2), beside)
    dense_y()
    lines = {}
    for p in (1, 0, 2):
        flows[p].wait()
        if p == 1:
            acc[p, x, own_half] = add_low(acc[p, x, own_half], from_x[p, own_half])
        else:
            acc[p, x, own_half] = add_low(acc[p, x, own_half], from_y[p, 0])
        for d in range(1, GROUPS):
            lines[p, d] = send(
                acc.at[p, x, piece_of(z ^ d)], from_z.at[p, d], pair(2 + d, p), line[d]
            )
    short.wait()
    vec[...] = vec[...] + vec_in[2]
    vec_in[4 + z] = vec[...]
    shorts = [
        send(vec, vec_in.at[4 + z], small_pair(2 + d), line[d]) for d in range(1, GROUPS)
    ]
    spread = {}
    for p in (1, 0, 2):
        total = acc[p, x, piece_of(z)].astype(F32)
        for d in range(1, GROUPS):
            lines[p, d].wait()
            total += from_z[p, d].astype(F32)
        res[c, p, piece_of(z)] = total.astype(BF16)
        for d in range(1, GROUPS):
            spread[p, d] = send(
                res.at[c, p, piece_of(z)],
                res.at[c, p, piece_of(z)],
                pair(5 + d, p),
                line[d],
            )
    for p in (1, 0, 2):
        for d in range(1, GROUPS):
            spread[p, d].wait()
        flows[p] = send(
            res.at[c, p, own_half], res.at[c, p, own_half], pair(9, p), beside
        )
    dense_core()
    for copy in shorts:
        copy.wait()
    small_out[...] = vec_in[4] + vec_in[5] + (vec_in[6] + vec_in[7])
    for p in (1, 0, 2):
        flows[p].wait()
        flows[p] = send(res.at[c, p], res.at[c, p], pair(10, p), sibling)
    for copy in dense_flows:
        copy.wait()
    done = [pltpu.make_async_copy(dense_res, dense_out, last_sem.at[1])]
    done[0].start()
    for p in (1, 0, 2):
        flows[p].wait()
    done.append(pltpu.make_async_copy(res, out, last_sem.at[0]))
    done[1].start()
    for copy in done:
        copy.wait()


def finish(lengths, order, tok, fg, rq, rkv, sums, wide_sums, ready, wq, wk, wv, others):
    seqs, _, width = tok.shape
    short = (-(-(9 * width + wide_sums.shape[1] + 128) // 1024) * 8, 128)
    parts, rows, lanes = 3, 3 * (width // 2), 128
    total, half = 8 * ready.shape[0], ready.shape[1]
    dma = pltpu.SemaphoreType.DMA
    return pl.pallas_call(
        functools.partial(finish_kernel, seqs),
        out_shape=[
            jax.ShapeDtypeStruct(tok.shape, F32),
            jax.ShapeDtypeStruct((2, parts, rows, lanes), BF16),
            jax.ShapeDtypeStruct((2, total, half), BF16),
            jax.ShapeDtypeStruct(short, F32),
        ],
        in_specs=[SMEM] * 2 + [VMEM] * 7 + [ANY] * 4,
        out_specs=[VMEM, ANY, ANY, VMEM],
        scratch_shapes=[
            pltpu.VMEM((3, width, width), BF16),
            pltpu.VMEM((parts, 2, 2, rows, lanes), BF16),
            pltpu.VMEM((parts, 2, rows, lanes), BF16),
            pltpu.VMEM((parts, 2, rows, lanes), BF16),
            pltpu.VMEM((parts, rows, lanes), BF16),
            pltpu.VMEM((parts, 2, rows // 2, lanes), BF16),
            pltpu.VMEM((parts, GROUPS, rows // 8, lanes), BF16),
            pltpu.VMEM((2, parts, rows, lanes), BF16),
            pltpu.VMEM(short, F32),
            pltpu.VMEM((9, *short), F32),
            pltpu.VMEM((2, total, half), BF16),
            dma((6,)),
            dma((2, 11, parts)),
            dma((2, 6)),
            dma((2, 4, 2)),
            dma((2,)),
        ],
        compiler_params=pltpu.CompilerParams(
            vmem_limit_bytes=63 * 2**20, collective_id=2, has_side_effects=True
        ),
        cost_estimate=cost(70),
        name="finish",
    )(lengths, order, tok, fg, rq, rkv, sums, wide_sums, ready, wq, wk, wv, others)


def unpack_kernel(qkv, total, *refs):
    outs, (narrow, inner, outer, sems) = refs[:6], refs[6:]
    half = qkv.shape[2] // 3
    blocks = inner.shape[1] // (2 * half)
    copies = []

    def leave(src, i):
        copy = pltpu.make_async_copy(src, outs[i], sems.at[i])
        copy.start()
        copies.append(copy)

    for k in range(2):
        cols = slice(k * half, (k + 1) * half)
        outer[:, cols] = total[k, (1 + blocks) * half :].astype(F32)
    leave(outer, 5)
    for k in range(2):
        for t in range(blocks):
            cols = slice((2 * t + k) * half, (2 * t + k + 1) * half)
            inner[:, cols] = total[k, (1 + t) * half : (2 + t) * half].astype(F32)
    leave(inner, 4)
    for i in range(3):
        for k in range(2):
            for p in range(3):
                cols = slice((3 * k + p) * 128, (3 * k + p + 1) * 128)
                narrow[i, :, cols] = qkv[k, p, i * half : (i + 1) * half].astype(F32)
        leave(narrow.at[i], i)
    for k in range(2):
        narrow[3, :, k * half : (k + 1) * half] = total[k, 0:half].astype(F32)
    leave(narrow.at[3], 3)
    for copy in copies:
        copy.wait()


def unpack(qkv, total, hidden):
    half = total.shape[2]
    narrow = jax.ShapeDtypeStruct((half, 2 * half), F32)
    return pl.pallas_call(
        unpack_kernel,
        out_shape=[narrow] * 4
        + [
            jax.ShapeDtypeStruct((half, hidden), F32),
            jax.ShapeDtypeStruct((hidden // 2, 2 * half), F32),
        ],
        in_specs=[VMEM] * 2,
        out_specs=[ANY] * 6,
        scratch_shapes=[
            pltpu.VMEM((4, half, 2 * half), F32),
            pltpu.VMEM((half, hidden), F32),
            pltpu.VMEM((hidden // 2, 2 * half), F32),
            pltpu.SemaphoreType.DMA((6,)),
        ],
        compiler_params=ROOM,
        cost_estimate=cost(10),
        name="unpack",
    )(qkv, total)


def pick(table, index):
    places = jnp.arange(table.shape[0], dtype=jnp.int32)
    return jnp.sum(jnp.where(index[..., None] == places, table, 0), -1)


def shards(
    size,
    tokens,
    teacher,
    lengths,
    block_order,
    query_weight,
    query_bias,
    key_weight,
    value_weight,
    value_bias,
    out_weight,
    out_bias,
    gain_one,
    shift_one,
    inner_weight,
    inner_bias,
    outer_weight,
    outer_bias,
    gain_two,
    shift_two,
):
    seqs, rows, width = tokens.shape
    per_plane = size // GROUPS
    blocks_each = rows // BLK
    ctx, x = lax.axis_index("ctx"), lax.axis_index("wa")
    c, place = lax.rem(ctx, 2), lax.rem(ctx, per_plane)
    masks = [1 << b for b in reversed(range(per_plane.bit_length() - 1))]
    offsets = [0]
    for m in masks:
        offsets += [o ^ m for o in offsets]

    def across(value):
        return lax.ppermute(value, "wa", [(0, 1), (1, 0)])

    def flip(value, m):
        return lax.ppermute(value, "ctx", [(i, i ^ m) for i in range(size)])

    lines = [[g * per_plane + r for g in range(GROUPS)] for r in range(per_plane)]

    def turn(value):
        return lax.all_to_all(value, "ctx", 0, 0, axis_index_groups=lines)

    cores = [[i for i in range(size) if i % 2 == k] for k in range(2)]

    def paired(mine):
        sibling = flip(mine, 1)
        return jnp.where(c == 0, jnp.stack([mine, sibling]), jnp.stack([sibling, mine]))

    def reduced(grad):
        four = grad.reshape(2, 2, *grad.shape[1:])
        keep = lax.dynamic_index_in_dim(four, c, 1, False)
        give = lax.dynamic_index_in_dim(four, 1 - c, 1, False)
        keep = add_low(keep, flip(give, 1))
        mine = lax.dynamic_index_in_dim(keep, x, 0, False)
        mine = add_low(mine, across(lax.dynamic_index_in_dim(keep, 1 - x, 0, False)))
        return paired(lax.psum(mine, "ctx", axis_index_groups=cores))

    def reduced_dense(grad):
        four = grad.reshape(2, 2, *grad.shape[1:])
        keep = lax.dynamic_index_in_dim(four, c, 1, False)
        give = lax.dynamic_index_in_dim(four, 1 - c, 1, False)
        keep = add_low(keep, flip(give, 1))
        mine = lax.psum_scatter(
            keep.reshape(-1, keep.shape[-1]), "wa", scatter_dimension=0, tiled=True
        )
        return lax.psum(mine, "ctx", axis_index_groups=cores)

    vectors = (
        query_bias,
        value_bias,
        out_bias,
        gain_one,
        shift_one,
        outer_bias,
        gain_two,
        shift_two,
        inner_bias,
    )
    half, hidden = width // 2, 2 * inner_bias.shape[0]
    fused = per_plane == 4

    if fused:
        found = start(
            lengths,
            block_order,
            tokens,
            (query_weight, key_weight, value_weight, out_weight, inner_weight, outer_weight),
            vectors,
        )
        queries = [q.reshape(-1, BLK, q.shape[2]) for q in found[:seqs]]
        pieces = [[kv.reshape(-1, BLK, kv.shape[3])] for kv in found[seqs : 2 * seqs]]
        attended, lses = found[2 * seqs : 3 * seqs], found[3 * seqs : 4 * seqs]
        first_back, pair, others, *rest = found[4 * seqs :]
        dense_weights = [out_weight, rest[0], inner_weight, rest[1], outer_weight, rest[2]]
    else:
        count = block_order.shape[0]
        ids = jnp.arange(count, dtype=jnp.int32)
        owner = ids // blocks_each
        index_of = jnp.array([offsets.index(o) for o in range(per_plane)], jnp.int32)
        piece_of = pick(index_of, (owner % per_plane) ^ place)
        spot = (piece_of * GROUPS + owner // per_plane) * blocks_each + ids % blocks_each
        key_order = jnp.sum(jnp.where(block_order[None, :] == ids[:, None], spot[None, :], 0), 1)
        near = jnp.arange(GROUPS * blocks_each, dtype=jnp.int32)
        near_ids = (near // blocks_each * per_plane + place) * blocks_each + near % blocks_each
        near_pos = pick(block_order, near_ids)
        rank = jnp.sum((near_pos[None, :] < near_pos[:, None]).astype(jnp.int32), 1)
        query_order = jnp.sum(jnp.where(rank[None, :] == near[:, None], near[None, :], 0), 1)
        own_pos = pick(block_order, ctx * blocks_each + jnp.arange(blocks_each, dtype=jnp.int32))
        scalars, row_counts = [], []
        for s in range(seqs):
            used = jnp.sum((near_pos * BLK < lengths[s]).astype(jnp.int32))
            head = jnp.concatenate([lengths[s][None], used[None], jnp.zeros((6,), jnp.int32)])
            scalars.append(jnp.concatenate([head, query_order, key_order]))
            row_counts.append(jnp.clip(lengths[s] - own_pos * BLK, 0, BLK))

        counts = jnp.concatenate(row_counts)
        own_vec = jnp.concatenate(vectors)[None]
        other_vec = across(own_vec)
        pair = jnp.where(
            x == 0, jnp.stack([own_vec, other_vec]), jnp.stack([other_vec, own_vec])
        ).astype(F32)
        narrow = pair[:, 0, : 8 * half].reshape(2, 8, half).swapaxes(0, 1).reshape(8, width)
        wide_vec = pair[:, 0, 8 * half :].reshape(1, -1)

        def quarter(weight):
            n = weight.shape[0] // 2
            return lax.dynamic_slice_in_dim(weight, c * n, n, 0)

        first_qkv = across(
            jnp.concatenate([quarter(w) for w in (query_weight, key_weight, value_weight)], 0)
        )
        second_qkv = flip(first_qkv, 1)
        dense_weights = []
        last = first_qkv
        for weight in (out_weight, inner_weight, outer_weight):
            piece, last = lax.optimization_barrier((quarter(weight), last))
            last = across(piece)
            dense_weights += [weight, last, flip(last, 1)]

        projected = project(
            counts, tokens, narrow, query_weight, key_weight, value_weight, first_qkv, second_qkv
        )
        queries, pieces = [], []
        for s in range(seqs):
            kv = turn(projected[2 * s + 1])
            queries.append(turn(projected[2 * s]).reshape(-1, BLK, width // GROUPS))
            held = [kv.reshape(-1, BLK, kv.shape[2])]
            for m in masks:
                held += [flip(piece, m) for piece in held]
            pieces.append(held)

        attended, lses = [], []
        for s in range(seqs):
            o, lse = attend(s, per_plane, lengths, block_order, queries[s], pieces[s])
            attended.append(o.reshape(queries[s].shape))
            lses.append(lse)
    if fused:
        fours = [first_back, *attended[1:]]
        found = middle(lengths, block_order, tokens, teacher, pair, fours, dense_weights)
        output, firsts, sums, wide_sums, a_own, a_give, b_own, b_give = found[:8]
        heads_grad = [g.reshape(queries[0].shape) for g in found[8:]]
        ready = (a_own, a_give, b_own, b_give)
    else:
        dense_out = []
        for s in range(seqs):
            o4 = turn(attended[s].reshape(GROUPS, rows, -1))
            dense_out.append(
                dense(
                    row_counts[s], o4, tokens[s], teacher[s], narrow[2:], wide_vec, dense_weights
                )
            )
        output = jnp.stack([d[0] for d in dense_out])
        first_grads = [d[1] for d in dense_out]
        heads_grad = [turn(d[2]).reshape(queries[s].shape) for s, d in enumerate(dense_out)]
        sums = sum(d[9] for d in dense_out)
        wide_sums = sum(d[10] for d in dense_out)
        dense_sums = [reduced_dense(g) for g in dense_grads([d[3:9] for d in dense_out])]

    if fused:
        flat_rows = (GROUPS * rows, width // GROUPS)
        rq, rkv, ready = attend_back_all(
            [
                [
                    *(a.reshape(flat_rows) for a in (queries[s], heads_grad[s], attended[s])),
                    lses[s],
                    pieces[s][0].reshape(-1, pieces[s][0].shape[2]),
                ]
                for s in range(seqs)
            ],
            ready,
        )
    else:
        dqs, dkvs = [], []
        for s in range(seqs):
            found = attend_back(
                scalars[s], queries[s], heads_grad[s], attended[s], lses[s], pieces[s]
            )
            dqs.append(turn(found[0].reshape(GROUPS, rows, -1)))
            held = [piece.reshape(GROUPS, rows, -1) for piece in found[1:]]
            for m in reversed(masks):
                n = len(held) // 2
                held = [add_low(mine, flip(theirs, m)) for mine, theirs in zip(held[:n], held[n:])]
            dkvs.append(turn(held[0]))
        tokens_grad, g_qkv, sums_qkv = project_grads(
            counts,
            tokens,
            first_grads,
            dqs + dkvs,
            query_weight,
            key_weight,
            value_weight,
            first_qkv,
            second_qkv,
        )

    if fused:
        tokens_grad, qkv, total, small = finish(
            lengths,
            block_order,
            tokens,
            firsts,
            rq,
            rkv,
            sums,
            wide_sums,
            ready,
            query_weight,
            key_weight,
            value_weight,
            others,
        )
        query_grad, key_grad, value_grad, out_grad, inner_grad, outer_grad = unpack(
            qkv, total, hidden
        )
        small = small.reshape(-1)
    else:
        valid = jnp.full((128,), sum(jnp.sum(r) for r in row_counts).astype(F32))
        small = jnp.concatenate(
            [sums[:7].reshape(-1), sums_qkv[:2].reshape(-1), wide_sums[0], valid]
        )
        small = lax.psum(small, ("ctx", "wa"))
        qkv = reduced(jnp.moveaxis(g_qkv, (2, 1), (0, 1)).reshape(4, 3, -1, 128))
        out_grad, inner_grad, outer_grad = (
            paired(g).reshape(-1, g.shape[-1]).astype(F32) for g in dense_sums
        )
        qkv = qkv.reshape(6, 3, half, 128).astype(F32)
        query_grad, key_grad, value_grad = (
            qkv[:, i].swapaxes(0, 1).reshape(half, width) for i in range(3)
        )

    def vector(start, length):
        return lax.dynamic_slice_in_dim(small, start + x * (length // 2), length // 2, 0)

    end = 9 * width
    loss = jnp.sum(small[6 * width : 7 * width]) / (small[end + hidden] * width)
    return (
        output,
        tokens_grad,
        query_grad,
        vector(7 * width, width),
        key_grad,
        value_grad,
        vector(8 * width, width),
        out_grad,
        vector(5 * width, width),
        vector(3 * width, width),
        vector(4 * width, width),
        inner_grad,
        vector(end, hidden),
        outer_grad,
        vector(2 * width, width),
        vector(0, width),
        vector(width, width),
        loss,
    )


def solution(mesh):
    row, split, both = P("wa"), P("wa", None), P("wa", "ctx", None)
    placed = (both, both, row, P(), split, row, split, split, row, split, row, row, row)
    placed += (split, row, split, row, row, row)
    return jax.shard_map(
        functools.partial(shards, mesh.shape["ctx"]),
        mesh=mesh,
        in_specs=placed,
        out_specs=(
            both,
            both,
            split,
            row,
            split,
            split,
            row,
            split,
            row,
            row,
            row,
            split,
            row,
            split,
            row,
            row,
            row,
            P(),
        ),
        check_vma=False,
    )
```

profile of v0, /device:TPU:0, one launch (start us, length us, event | category | flops | bytes accessed | tf_op | source)
XLA Modules:
  0.0 381.4 jit_solution(13452877080183224473)
XLA Ops:
  0.7 118.3 %start.1 = (bf16[4,256,192]{2,1,0:T(8,128)(2,1)}, bf16[4,256,192]{2,1,0:T(8,128)(2,1)}, bf16[4,4,256,384]{3,2,1,0:T(8,128)(2,1)}, bf16[4,4,256,384]{3,2,1,0:T(8,...) custom-call(s32[2]{0:T(128)} %lengths.5, ...), custom_call_target="tpu_custom_call" | custom-call | flops 92000002048 | bytes 1048576 | tf_op jit(solution)/shard_map/start/pallas_call | solution.py:1197
  119.0 51.3 %middle.1 = (bf16[2,256,768]{2,1,0:T(8,128)(2,1)}, f32[2,256,768]{2,1,0:T(8,128)}, f32[8,768]{1,0:T(8,128)}, f32[1,3072]{1,0:T(1,128)}, bf16[1664,384]{1,0:T(8,1...) custom-call(s32[2]{0:T(128)} %lengths.5, ...), custom_call_target="tpu_custom_call" | custom-call | flops 69000003584 | bytes 1048576 | tf_op jit(solution)/shard_map/middle/pallas_call | solution.py:1440
  170.2 121.3 %attend_back_all.1 = (bf16[3,4,256,128]{3,2,1,0:T(8,128)(2,1)}, bf16[6,4,256,128]{3,2,1,0:T(8,128)(2,1)}, bf16[432,384]{1,0:T(8,128)(2,1)}) custom-call(bf16[1024,192]{1,0:T(8,128)(2,1)} %bitcast.15, bf16[1024,192]{1,0:T(8,128)(2,1)} %bitcast.19, bf16[1024,192]{1,0:T(8,128)(2,1)} %bitcast.17, f32[3,8,1024]{2,1,0:T(8,128)} %get-tuple-element.66.refs_3_, ...), custom_call_target="tpu_custom_call" | custom-call | flops 138000007168 | bytes 1048576 | tf_op jit(solution)/shard_map/attend_back_all/pallas_call | solution.py:868
  291.5 72.8 %finish.1 = (f32[2,256,768]{2,1,0:T(8,128)}, bf16[2,3,1152,128]{3,2,1,0:T(8,128)(2,1)}, bf16[2,3456,384]{2,1,0:T(8,128)(2,1)}, f32[80,128]{1,0:T(8,128)}) custom-call(s32[2]{0:T(128)} %lengths.5, s32[32]{0:T(128)} %order.5, bf16[2,256,768]{2,1,0:T(8,128)(2,1)} %tok.3, f32[2,256,768]{2,1,0:T(8,128)} %get-tuple-element.62.fg, ...), custom_call_target="tpu_custom_call" | custom-call | flops 80499998720 | bytes 1048576 | tf_op jit(solution)/shard_map/finish/pallas_call | solution.py:1684
  364.3 1.2 slice.9
  366.1 1.3 slice_reduce_fusion
  368.1 0.0 copy-start.2
  368.1 0.0 copy-start.1
  368.1 8.5 %unpack.1 = (f32[384,768]{1,0:T(8,128)}, f32[384,768]{1,0:T(8,128)}, f32[384,768]{1,0:T(8,128)}, f32[384,768]{1,0:T(8,128)}, f32[384,3072]{1,0:T(8,128)}, /*index=5*/f32[1536,768]{1,0:T(8,128)}) custom-call(bf16[2,3,1152,128]{3,2,1,0:T(8,128)(2,1)} %get-tuple-element.83.qkv, bf16[2,3456,384]{2,1,0:T(8,128)(2,1)} %get-tuple-element.84.total), custom_call_target="tpu_custom_call" | custom-call | flops 11500000256 | bytes 1048576 | tf_op jit(solution)/shard_map/unpack/pallas_call | solution.py:1756
  376.6 0.0 copy-start
  376.7 0.0 copy-done.2
  376.7 0.7 fusion
  377.4 0.7 dynamic_slice.32
  378.0 0.0 copy-done.1
  378.0 0.9 copy.39
  378.9 0.0 copy-done
  378.9 1.1 copy.40
Async XLA Ops:
  368.1 8.6 %copy-start.2 = (f32[80,128]{1,0:T(8,128)S(1)}, f32[80,128]{1,0:T(8,128)}, u32[]{:S(2)}) copy-start(f32[80,128]{1,0:T(8,128)} %get-tuple-element.86) | copy-start | bytes 122884
  368.1 9.9 %copy-start.1 = (bf16[2,256,768]{2,1,0:T(8,128)(2,1)S(1)}, bf16[2,256,768]{2,1,0:T(8,128)(2,1)}, u32[]{:S(2)}) copy-start(bf16[2,256,768]{2,1,0:T(8,128)(2,1)} %get-tuple-element.118) | copy-start | bytes 2359300
  376.6 2.3 copy-start
where the time goes:
time: 384 us; the launch traced here: 381 us
  Pallas kernels  372 us (97%)
  local copies, waits for them, and re-layouts  4.59 us (1%)
    pallas_call x1, Pallas kernels, attend_back_all(): pl.pallas_call(functools.partial(back_kernel, seqs), out_shape=[jax.Shape...  121 us
    pallas_call x1, Pallas kernels, start(): pl.pallas_call(functools.partial(start_kernel, seqs), out_shape=[narrow]...  118 us
    pallas_call x1, Pallas kernels, finish(): pl.pallas_call(functools.partial(finish_kernel, seqs), out_shape=[jax.Sha...  72.8 us
    pallas_call x1, Pallas kernels, middle(): pl.pallas_call(functools.partial(middle_kernel, seqs), out_shape=[jax.Sha...  51.3 us
    pallas_call x1, Pallas kernels, unpack(): pl.pallas_call(unpack_kernel, out_shape=[narrow] * 4 + [jax.ShapeDtypeStr...  8.52 us

commit v1 on v0

--- a/solution.py
+++ b/solution.py
@@ -1096,7 +1096,7 @@
 
     def attend_part(s, h, pieces):
         lanes = slice(h * 128, (h + 1) * 128)
-        count, tile = GROUPS * rows, 256
+        count, tile = GROUPS * rows, 1024
 
         def step(j, _):
             piece = pieces[0] + j * (pieces[1] - pieces[0])
@@ -1503,31 +1503,21 @@
     def d_pair(k, i):
         return d_sems.at[0, k, i], d_sems.at[1, k, i]
 
-    dense_flows = []
-    for i, (start, n, base) in enumerate(dense_parts):
-        place = dense_rows(base + low_bit * (n // 2) + high_bit * (n // 4), n // 4)
-        src = ready.at[start : start + n // 4]
-        place[...] = src[...]
-        dense_flows.append(send(src, place, d_pair(0, i), line[2]))
-
-    def dense_near():
-        for i, (_, n, base) in enumerate(dense_parts):
+    dense_flows = [None, None]
+
+    def dense_step(i, k):
+        start, n, base = dense_parts[i]
+        if k > 0:
             dense_flows[i].wait()
-            place = dense_rows(base + low_bit * (n // 2), n // 2)
-            dense_flows[i] = send(place, place, d_pair(1, i), line[1])
-
-    def dense_y():
-        for i, (_, n, base) in enumerate(dense_parts):
-            dense_flows[i].wait()
-            place = dense_rows(base, n)
-            dense_flows[i] = send(place, place, d_pair(2, i), beside)
-
-    def dense_core():
-        for i, (_, n, _) in enumerate(dense_parts):
-            dense_flows[i].wait()
-            place = dense_res.at[c, pl.ds(2 * a_half * i, 2 * n)]
-            dense_flows[i] = send(place, place, d_pair(3, i), sibling)
-
+        begin = base + (low_bit * (n // 2) if k < 2 else 0) + (high_bit * (n // 4) if k < 1 else 0)
+        size = (n // 4, n // 2, n, 2 * n)[k]
+        place = dense_rows(begin if k < 3 else 2 * a_half * i, size)
+        if k == 0:
+            place[...] = ready[start : start + size]
+        to = (line[2], line[1], beside, sibling)[k]
+        dense_flows[i] = send(place, place, d_pair(k, i), to)
+
+    dense_step(0, 0)
     rows, width = tok.shape[1:]
     heads = width // GROUPS // DH
     copies = []
@@ -1588,81 +1578,119 @@
         send(grads.at[p, 1 - c], from_core.at[p], pair(0, p), sibling) for p in range(parts)
     ]
     short = send(vec, vec_in.at[0], small_pair(0), sibling)
-    flows = []
-    for p in range(parts):
+    flows, lines, spread = {}, {}, {}
+
+    def from_pair(p):
         core[p].wait()
         acc[p] = add_low(grads[p, c], from_core[p])
+
+    def x_send(p):
         if p == 1:
-            flows.append(send(acc.at[p, :, other_half], from_y.at[p], pair(1, p), beside))
+            flows[p] = send(acc.at[p, 1 - x, own_half], from_x.at[p, own_half], pair(2, p), over)
         else:
-            flows.append(send(acc.at[p, 1 - x], from_x.at[p], pair(1, p), over))
-    dense_near()
+            flows[p] = send(acc.at[p, 1 - x], from_x.at[p], pair(1, p), over)
+
+    def x_add(p):
+        flows[p].wait()
+        if p == 1:
+            acc[p, x, own_half] = add_low(acc[p, x, own_half], from_x[p, own_half])
+        else:
+            acc[p, x] = add_low(acc[p, x], from_x[p])
+
+    def y_send(p):
+        if p == 1:
+            flows[p] = send(acc.at[p, :, other_half], from_y.at[p], pair(1, p), beside)
+        else:
+            flows[p] = send(acc.at[p, x, other_half], from_y.at[p, 0], pair(2, p), beside)
+
+    def y_add(p):
+        flows[p].wait()
+        if p == 1:
+            for k in range(2):
+                acc[p, k, own_half] = add_low(acc[p, k, own_half], from_y[p, k])
+        else:
+            acc[p, x, own_half] = add_low(acc[p, x, own_half], from_y[p, 0])
+
+    def z_send(p):
+        for d in range(1, GROUPS):
+            lines[p, d] = send(
+                acc.at[p, x, piece_of(z ^ d)], from_z.at[p, d], pair(2 + d, p), line[d]
+            )
+
+    def z_add(p):
+        total = acc[p, x, piece_of(z)].astype(F32)
+        for d in range(1, GROUPS):
+            lines[p, d].wait()
+            total += from_z[p, d].astype(F32)
+        place = res.at[c, p, piece_of(z)]
+        place[...] = total.astype(BF16)
+        for d in range(1, GROUPS):
+            spread[p, d] = send(place, place, pair(5 + d, p), line[d])
+
+    def y_gather(p):
+        for d in range(1, GROUPS):
+            spread[p, d].wait()
+        place = res.at[c, p, own_half]
+        flows[p] = send(place, place, pair(9, p), beside)
+
+    def core_gather(p):
+        flows[p].wait()
+        flows[p] = send(res.at[c, p], res.at[c, p], pair(10, p), sibling)
+
+    from_pair(0)
+    x_send(0)
+    from_pair(1)
+    y_send(1)
+    from_pair(2)
+    short.wait()
+    vec_in[8] = vec[...] + vec_in[0]
+    short = send(vec_in.at[8], vec_in.at[1], small_pair(1), over)
+    dense_step(0, 1)
+    dense_step(1, 0)
     for copy in copies:
         copy.wait()
     total = jnp.concatenate([fg[s] for s in range(seqs)], 0)
     for i, grad in enumerate(parted):
         total += dot(grad, full[i], NT)
     tg[...] = total.reshape(seqs, rows, width)
-    short.wait()
-    vec_in[8] = vec[...] + vec_in[0]
-    short = send(vec_in.at[8], vec_in.at[1], small_pair(1), over)
-    for p in (1, 0, 2):
-        flows[p].wait()
-        if p == 1:
-            for k in range(2):
-                acc[p, k, own_half] = add_low(acc[p, k, own_half], from_y[p, k])
-            flows[p] = send(acc.at[p, 1 - x, own_half], from_x.at[p, own_half], pair(2, p), over)
-        else:
-            acc[p, x] = add_low(acc[p, x], from_x[p])
-            flows[p] = send(acc.at[p, x, other_half], from_y.at[p, 0], pair(2, p), beside)
+    x_add(0)
+    x_send(2)
+    y_send(0)
+    y_add(1)
+    x_send(1)
     short.wait()
     vec[...] = vec_in[8] + vec_in[1]
     short = send(vec, vec_in.at[2], small_pair(2), beside)
-    dense_y()
-    lines = {}
-    for p in (1, 0, 2):
-        flows[p].wait()
-        if p == 1:
-            acc[p, x, own_half] = add_low(acc[p, x, own_half], from_x[p, own_half])
-        else:
-            acc[p, x, own_half] = add_low(acc[p, x, own_half], from_y[p, 0])
-        for d in range(1, GROUPS):
-            lines[p, d] = send(
-                acc.at[p, x, piece_of(z ^ d)], from_z.at[p, d], pair(2 + d, p), line[d]
-            )
+    y_add(0)
+    z_send(0)
+    dense_step(0, 2)
+    dense_step(1, 1)
+    x_add(2)
+    y_send(2)
+    x_add(1)
+    z_send(1)
+    z_add(0)
     short.wait()
     vec[...] = vec[...] + vec_in[2]
     vec_in[4 + z] = vec[...]
     shorts = [
         send(vec, vec_in.at[4 + z], small_pair(2 + d), line[d]) for d in range(1, GROUPS)
     ]
-    spread = {}
-    for p in (1, 0, 2):
-        total = acc[p, x, piece_of(z)].astype(F32)
-        for d in range(1, GROUPS):
-            lines[p, d].wait()
-            total += from_z[p, d].astype(F32)
-        res[c, p, piece_of(z)] = total.astype(BF16)
-        for d in range(1, GROUPS):
-            spread[p, d] = send(
-                res.at[c, p, piece_of(z)],
-                res.at[c, p, piece_of(z)],
-                pair(5 + d, p),
-                line[d],
-            )
-    for p in (1, 0, 2):
-        for d in range(1, GROUPS):
-            spread[p, d].wait()
-        flows[p] = send(
-            res.at[c, p, own_half], res.at[c, p, own_half], pair(9, p), beside
-        )
-    dense_core()
+    y_add(2)
+    z_send(2)
+    dense_step(1, 2)
+    z_add(1)
+    y_gather(0)
+    z_add(2)
+    dense_step(0, 3)
+    y_gather(1)
+    y_gather(2)
     for copy in shorts:
         copy.wait()
     small_out[...] = vec_in[4] + vec_in[5] + (vec_in[6] + vec_in[7])
-    for p in (1, 0, 2):
-        flows[p].wait()
-        flows[p] = send(res.at[c, p], res.at[c, p], pair(10, p), sibling)
+    for p in range(parts):
+        core_gather(p)
+    dense_step(1, 3)
     for copy in dense_flows:
         copy.wait()
     done = [pltpu.make_async_copy(dense_res, dense_out, last_sem.at[1])]
@@ -1717,8 +1745,9 @@
     )(lengths, order, tok, fg, rq, rkv, sums, wide_sums, ready, wq, wk, wv, others)
 
 
-def unpack_kernel(qkv, total, *refs):
-    outs, (narrow, inner, outer, sems) = refs[:6], refs[6:]
+def unpack_kernel(qkv, total, small, *refs):
+    outs, rows, loss, refs = refs[:6], refs[6:15], refs[15], refs[16:]
+    narrow, inner, outer, sems = refs
     half = qkv.shape[2] // 3
     blocks = inner.shape[1] // (2 * half)
     copies = []
@@ -1746,11 +1775,21 @@
     for k in range(2):
         narrow[3, :, k * half : (k + 1) * half] = total[k, 0:half].astype(F32)
     leave(narrow.at[3], 3)
+    x = lax.axis_index("wa")
+    tiles = 2 * half // 128
+    starts = [tiles * i for i in (0, 1, 2, 3, 4, 5, 7, 8)] + [9 * tiles]
+    for one, begin in zip(rows, starts):
+        n = one.shape[0] // 128
+        for t in range(n):
+            one[t * 128 : (t + 1) * 128] = small[pl.ds(begin + x * n + t, 1), :][0]
+    end = 9 * tiles + 2 * rows[8].shape[0] // 128
+    squares = jnp.sum(small[6 * tiles : 7 * tiles, :], keepdims=True)
+    loss[...] = squares / (small[end : end + 1, :1] * (2.0 * half))
     for copy in copies:
         copy.wait()
 
 
-def unpack(qkv, total, hidden):
+def unpack(qkv, total, small, hidden):
     half = total.shape[2]
     narrow = jax.ShapeDtypeStruct((half, 2 * half), F32)
     return pl.pallas_call(
@@ -1759,9 +1798,11 @@
         + [
             jax.ShapeDtypeStruct((half, hidden), F32),
             jax.ShapeDtypeStruct((hidden // 2, 2 * half), F32),
-        ],
-        in_specs=[VMEM] * 2,
-        out_specs=[ANY] * 6,
+        ]
+        + [jax.ShapeDtypeStruct((half,), F32)] * 8
+        + [jax.ShapeDtypeStruct((hidden // 2,), F32), jax.ShapeDtypeStruct((1, 1), F32)],
+        in_specs=[VMEM] * 3,
+        out_specs=[ANY] * 6 + [VMEM] * 10,
         scratch_shapes=[
             pltpu.VMEM((4, half, 2 * half), F32),
             pltpu.VMEM((half, hidden), F32),
@@ -1771,7 +1812,7 @@
         compiler_params=ROOM,
         cost_estimate=cost(10),
         name="unpack",
-    )(qkv, total)
+    )(qkv, total, small)
 
 
 def pick(table, index):
@@ -2011,10 +2052,14 @@
             value_weight,
             others,
         )
-        query_grad, key_grad, value_grad, out_grad, inner_grad, outer_grad = unpack(
-            qkv, total, hidden
-        )
-        small = small.reshape(-1)
+        grads = unpack(qkv, total, small, hidden)
+        query_grad, key_grad, value_grad, out_grad, inner_grad, outer_grad = grads[:6]
+        rows_of = dict(zip((0, 1, 2, 3, 4, 5, 7, 8, 9), grads[6:15]))
+        loss = grads[15].reshape(())
+
+        def vector(start, length):
+            return rows_of[start // width]
+
     else:
         valid = jnp.full((128,), sum(jnp.sum(r) for r in row_counts).astype(F32))
         small = jnp.concatenate(
@@ -2030,11 +2075,12 @@
             qkv[:, i].swapaxes(0, 1).reshape(half, width) for i in range(3)
         )
 
-    def vector(start, length):
-        return lax.dynamic_slice_in_dim(small, start + x * (length // 2), length // 2, 0)
+        def vector(start, length):
+            return lax.dynamic_slice_in_dim(small, start + x * (length // 2), length // 2, 0)
+
+        loss = jnp.sum(small[6 * width : 7 * width]) / (small[9 * width + hidden] * width)
 
     end = 9 * width
-    loss = jnp.sum(small[6 * width : 7 * width]) / (small[end + hidden] * width)
     return (
         output,
         tokens_grad,

time: 384 us -> 371 us (0.966)
  Pallas kernels: 372 us -> 364 us
    pallas_call x1, Pallas kernels: 118 us -> 108 us  [start(): pl.pallas_call(functools.partial(start_kernel, seqs), out_shape=[narrow]...]
where the time goes in v1:
time: 371 us; the launch traced here: 368 us
  Pallas kernels  364 us (98%)
    pallas_call x1, Pallas kernels, attend_back_all(): pl.pallas_call(functools.partial(back_kernel, seqs), out_shape=[jax.Shape...  121 us
    pallas_call x1, Pallas kernels, start(): pl.pallas_call(functools.partial(start_kernel, seqs), out_shape=[narrow]...  108 us
    pallas_call x1, Pallas kernels, finish(): pl.pallas_call(functools.partial(finish_kernel, seqs), out_shape=[jax.Sha...  74.4 us
    pallas_call x1, Pallas kernels, middle(): pl.pallas_call(functools.partial(middle_kernel, seqs), out_shape=[jax.Sha...  51.2 us
    pallas_call x1, Pallas kernels, unpack(): pl.pallas_call(unpack_kernel, out_shape=[narrow] * 4 + [jax.ShapeDtypeStr...  9.19 us

profile of v1, /device:TPU:0, one launch (start us, length us, event | category | flops | bytes accessed | tf_op | source)
XLA Modules:
  0.0 367.6 jit_solution(5319537496296631925)
XLA Ops:
  0.7 108.0 %start.1 = (bf16[4,256,192]{2,1,0:T(8,128)(2,1)}, bf16[4,256,192]{2,1,0:T(8,128)(2,1)}, bf16[4,4,256,384]{3,2,1,0:T(8,128)(2,1)}, bf16[4,4,256,384]{3,2,1,0:T(8,...) custom-call(s32[2]{0:T(128)} %lengths.5, ...), custom_call_target="tpu_custom_call" | custom-call | flops 92000002048 | bytes 1048576 | tf_op jit(solution)/shard_map/start/pallas_call | solution.py:1197
  108.7 51.2 %middle.1 = (bf16[2,256,768]{2,1,0:T(8,128)(2,1)}, f32[2,256,768]{2,1,0:T(8,128)}, f32[8,768]{1,0:T(8,128)}, f32[1,3072]{1,0:T(1,128)}, bf16[1664,384]{1,0:T(8,1...) custom-call(s32[2]{0:T(128)} %lengths.5, ...), custom_call_target="tpu_custom_call" | custom-call | flops 69000003584 | bytes 1048576 | tf_op jit(solution)/shard_map/middle/pallas_call | solution.py:1440
  159.9 120.9 %attend_back_all.1 = (bf16[3,4,256,128]{3,2,1,0:T(8,128)(2,1)}, bf16[6,4,256,128]{3,2,1,0:T(8,128)(2,1)}, bf16[432,384]{1,0:T(8,128)(2,1)}) custom-call(bf16[1024,192]{1,0:T(8,128)(2,1)} %bitcast.11, bf16[1024,192]{1,0:T(8,128)(2,1)} %bitcast.15, bf16[1024,192]{1,0:T(8,128)(2,1)} %bitcast.13, f32[3,8,1024]{2,1,0:T(8,128)} %get-tuple-element.76.refs_3_, ...), custom_call_target="tpu_custom_call" | custom-call | flops 138000007168 | bytes 1048576 | tf_op jit(solution)/shard_map/attend_back_all/pallas_call | solution.py:868
  280.8 74.4 %finish.1 = (f32[2,256,768]{2,1,0:T(8,128)}, bf16[2,3,1152,128]{3,2,1,0:T(8,128)(2,1)}, bf16[2,3456,384]{2,1,0:T(8,128)(2,1)}, f32[80,128]{1,0:T(8,128)}) custom-call(s32[2]{0:T(128)} %lengths.5, s32[32]{0:T(128)} %order.5, bf16[2,256,768]{2,1,0:T(8,128)(2,1)} %tok.3, f32[2,256,768]{2,1,0:T(8,128)} %get-tuple-element.72.fg, ...), custom_call_target="tpu_custom_call" | custom-call | flops 80499998720 | bytes 1048576 | tf_op jit(solution)/shard_map/finish/pallas_call | solution.py:1712
  355.3 0.0 copy-start.1
  355.3 9.2 %unpack.1 = (f32[384,768]{1,0:T(8,128)}, f32[384,768]{1,0:T(8,128)}, f32[384,768]{1,0:T(8,128)}, f32[384,768]{1,0:T(8,128)}, f32[384,3072]{1,0:T(8,128)}, /*inde...) custom-call(bf16[2,3,1152,128]{3,2,1,0:T(8,128)(2,1)} %get-tuple-ele, ...), custom_call_target="tpu_custom_call" | custom-call | flops 11500000256 | bytes 1048576 | tf_op jit(solution)/shard_map/unpack/pallas_call | solution.py:1795
  364.5 0.0 copy-start
  364.5 0.0 copy-done.1
  364.5 0.9 copy.39
  365.4 0.8 copy-done
  366.2 1.1 copy.40
Async XLA Ops:
  355.3 9.2 %copy-start.1 = (bf16[2,256,768]{2,1,0:T(8,128)(2,1)S(1)}, bf16[2,256,768]{2,1,0:T(8,128)(2,1)}, u32[]{:S(2)}) copy-start(bf16[2,256,768]{2,1,0:T(8,128)(2,1)} %get-tuple-element.130) | copy-start | bytes 2359300
  364.5 1.7 copy-start

commit v2 on v1

--- a/solution.py
+++ b/solution.py
@@ -1070,7 +1070,6 @@
     copy = pltpu.make_async_copy(vec, vec_out, l_sem.at[7])
     copy.start()
     waits.append(copy)
-    q_sends(0)
     for s in range(seqs):
         kv_v[s, 0, z] = kv_held[s, z]
         q_v[s, z] = q_held[s, z]
@@ -1104,20 +1103,20 @@
             dark = shade[s, piece, 0:1, :]
             for n in range(count // tile):
                 part = slice(n * tile, (n + 1) * tile)
-                scores = dot(qa[part, :], kv, NT) + dark
+                scores = dot(qa[h, part, :], kv, NT) + dark
                 high = scores[:, :128]
                 for i in range(1, count // 128):
                     high = jnp.maximum(high, scores[:, i * 128 : (i + 1) * 128])
-                old = top[part, :]
+                old = top[h, part, :]
                 new = jnp.maximum(old, jnp.max(high, 1, keepdims=True))
                 fade = jnp.exp2(old - new)
                 each = [
                     jnp.exp2(scores[:, i * 128 : (i + 1) * 128] - new) for i in range(count // 128)
                 ]
-                sums[part, :] = sums[part, :] * fade + sum(each)
+                sums[h, part, :] = sums[h, part, :] * fade + sum(each)
                 p = jnp.concatenate([one.astype(BF16) for one in each], 1)
-                acc[part, :] = acc[part, :] * fade + dot(p, kv)
-                top[part, :] = new
+                acc[h, part, :] = acc[h, part, :] * fade + dot(p, kv)
+                top[h, part, :] = new
             return 0
 
         lax.fori_loop(0, 2, step, 0)
@@ -1125,63 +1124,69 @@
     def attend_begin(s, h):
         hs = slice(h * DH, (h + 1) * DH)
         mine = q_v[s, :, :, hs].reshape(GROUPS * rows, DH)
-        qa[...] = jnp.concatenate([mine, jnp.zeros_like(mine)], 1)
-        acc[...] = jnp.zeros_like(acc)
-        sums[...] = jnp.zeros_like(sums)
-        top[...] = jnp.full_like(top, -1e30)
+        qa[h] = jnp.concatenate([mine, jnp.zeros_like(mine)], 1)
+        zero = jnp.zeros(acc.shape[1:], F32)
+        acc[h], sums[h], top[h] = zero, zero, zero - 1e30
 
     def attend_end(s, h):
         hs = slice(h * DH, (h + 1) * DH)
-        total = jnp.sum(sums[...], 1, keepdims=True)
-        logs = top[...] + jnp.log2(jnp.broadcast_to(total, top.shape))
+        total = jnp.sum(sums[h], 1, keepdims=True)
+        logs = top[h] + jnp.log2(jnp.broadcast_to(total, top.shape[1:]))
         lse_v[s, h] = jnp.transpose(logs)[:8]
-        found = (acc[:, DH:] * (1.0 / total)).astype(BF16)
+        found = (acc[h][:, DH:] * (1.0 / total)).astype(BF16)
         o_v[s, :, :, hs] = found.reshape(GROUPS, rows, DH)
+
+    def leave_all(s):
+        for i, (src, dst) in enumerate(
+            ((q_v, q_out), (kv_v, kv_out), (o_v, o_out), (lse_v, lse_out))
+        ):
+            leave(src.at[s], dst[s], 4 * s + i)
 
     for d in range(1, GROUPS):
         arrive(0, d)
         if d > 1:
             pass_core(0, d - 2)
-    kv_sends(1)
-    pass_on(1, 0, kv_held.at[1, z])
+    q_sends(0)
     pass_core(0, 2)
     pass_core(0, 3)
     for d in range(1, GROUPS):
         flow["q", 0, d].wait()
-    q_sends(1)
+    kv_sends(1)
     own_and_core(0)
-    slots = {
-        2: (lambda: pass_core(1, 0), lambda: arrive(1, 1)),
-        3: (lambda: arrive(1, 2), lambda: arrive(1, 3)),
-        4: (lambda: pass_core(1, 1), lambda: dense_core(0)),
-        5: (lambda: pass_core(1, 2),),
-        6: (lambda: own_and_core(1), lambda: [flow["q", 1, d].wait() for d in range(1, GROUPS)]),
-        7: (lambda: pass_core(1, 3),),
-        8: (lambda: dense_core(1),),
-        10: (lambda: dense_core(2),),
-    }
-    for s in range(seqs):
-        for h in range(heads):
-            for n, pieces in enumerate(((0, 2), (1, 3))):
-                for work in slots.get(6 * s + 2 * h + n, ()):
-                    work()
-                if n == 0:
-                    attend_begin(s, h)
-                if h == 0 and n == 1:
-                    for d in range(GROUPS):
-                        flow["kc", s, d, 1].wait()
-                attend_part(s, h, pieces)
-            attend_end(s, h)
-        if s == 0:
+    pass_on(1, 0, kv_held.at[1, z])
+    for d in range(GROUPS):
+        flow["kc", 0, d, 1].wait()
+    for h in range(heads):
+        attend_begin(0, h)
+        attend_part(0, h, (0, 2))
+        if h == 1:
+            dense_core(0)
+        if h == 2:
+            pass_core(1, 0)
+            q_sends(1)
             for d in range(1, GROUPS):
-                waits.append(
-                    send(o_v.at[0, z ^ d], back_out.at[z], pair(own_sem, d), line[d])
-                )
-            leave(o_v.at[0, z], back_out.at[z], 4 * seqs)
-        for i, (src, dst) in enumerate(
-            ((q_v, q_out), (kv_v, kv_out), (o_v, o_out), (lse_v, lse_out))
-        ):
-            leave(src.at[s], dst[s], 4 * s + i)
+                arrive(1, d)
+        attend_part(0, h, (1, 3))
+        attend_end(0, h)
+    leave_all(0)
+    own_and_core(1)
+    for d in range(1, GROUPS):
+        flow["q", 1, d].wait()
+    for d in range(1, GROUPS):
+        waits.append(send(o_v.at[0, z ^ d], back_out.at[z], pair(own_sem, d), line[d]))
+    leave(o_v.at[0, z], back_out.at[z], 4 * seqs)
+    for h in range(heads):
+        attend_begin(1, h)
+        attend_part(1, h, (0, 2))
+        pass_core(1, h + 1)
+    dense_core(1)
+    dense_core(2)
+    for d in range(GROUPS):
+        flow["kc", 1, d, 1].wait()
+    for h in range(heads):
+        attend_part(1, h, (1, 3))
+        attend_end(1, h)
+    leave_all(1)
     for copy in waits:
         copy.wait()
 
@@ -1220,10 +1225,10 @@
             pltpu.VMEM((seqs, GROUPS, rows, per), BF16),
             pltpu.VMEM((seqs, heads, 8, total), F32),
             pltpu.VMEM((seqs, 4, 8, total), F32),
-            pltpu.VMEM((total, 128), BF16),
-            pltpu.VMEM((total, 128), F32),
-            pltpu.VMEM((total, 128), F32),
-            pltpu.VMEM((total, 128), F32),
+            pltpu.VMEM((heads, total, 128), BF16),
+            pltpu.VMEM((heads, total, 128), F32),
+            pltpu.VMEM((heads, total, 128), F32),
+            pltpu.VMEM((heads, total, 128), F32),
             dma((2,)),
             dma((2, 3)),
             dma((2, 3)),

time: 371 us -> 366 us (0.987)
  Pallas kernels: 364 us -> 359 us
where the time goes in v2:
time: 366 us; the launch traced here: 363 us
  Pallas kernels  359 us (98%)
    pallas_call x1, Pallas kernels, attend_back_all(): pl.pallas_call(functools.partial(back_kernel, seqs), out_shape=[jax.Shape...  120 us
    pallas_call x1, Pallas kernels, start(): pl.pallas_call(functools.partial(start_kernel, seqs), out_shape=[narrow]...  106 us
    pallas_call x1, Pallas kernels, finish(): pl.pallas_call(functools.partial(finish_kernel, seqs), out_shape=[jax.Sha...  76.9 us
    pallas_call x1, Pallas kernels, middle(): pl.pallas_call(functools.partial(middle_kernel, seqs), out_shape=[jax.Sha...  47.8 us
    pallas_call x1, Pallas kernels, unpack(): pl.pallas_call(unpack_kernel, out_shape=[narrow] * 4 + [jax.ShapeDtypeStr...  9.19 us

profile of v2, /device:TPU:0, one launch (start us, length us, event | category | flops | bytes accessed | tf_op | source)
XLA Modules:
  0.0 363.1 jit_solution(7541947274284140819)
XLA Ops:
  0.7 105.8 %start.1 = (bf16[4,256,192]{2,1,0:T(8,128)(2,1)}, bf16[4,256,192]{2,1,0:T(8,128)(2,1)}, bf16[4,4,256,384]{3,2,1,0:T(8,128)(2,1)}, bf16[4,4,256,384]{3,2,1,0:T(8,...) custom-call(s32[2]{0:T(128)} %lengths.5, ...), custom_call_target="tpu_custom_call" | custom-call | flops 92000002048 | bytes 1048576 | tf_op jit(solution)/shard_map/start/pallas_call | solution.py:1202
  106.5 47.8 %middle.1 = (bf16[2,256,768]{2,1,0:T(8,128)(2,1)}, f32[2,256,768]{2,1,0:T(8,128)}, f32[8,768]{1,0:T(8,128)}, f32[1,3072]{1,0:T(1,128)}, bf16[1664,384]{1,0:T(8,1...) custom-call(s32[2]{0:T(128)} %lengths.5, ...), custom_call_target="tpu_custom_call" | custom-call | flops 69000003584 | bytes 1048576 | tf_op jit(solution)/shard_map/middle/pallas_call | solution.py:1445
  154.3 119.6 %attend_back_all.1 = (bf16[3,4,256,128]{3,2,1,0:T(8,128)(2,1)}, bf16[6,4,256,128]{3,2,1,0:T(8,128)(2,1)}, bf16[432,384]{1,0:T(8,128)(2,1)}) custom-call(bf16[1024,192]{1,0:T(8,128)(2,1)} %bitcast.11, bf16[1024,192]{1,0:T(8,128)(2,1)} %bitcast.15, bf16[1024,192]{1,0:T(8,128)(2,1)} %bitcast.13, f32[3,8,1024]{2,1,0:T(8,128)} %get-tuple-element.76.refs_3_, ...), custom_call_target="tpu_custom_call" | custom-call | flops 138000007168 | bytes 1048576 | tf_op jit(solution)/shard_map/attend_back_all/pallas_call | solution.py:868
  273.9 76.9 %finish.1 = (f32[2,256,768]{2,1,0:T(8,128)}, bf16[2,3,1152,128]{3,2,1,0:T(8,128)(2,1)}, bf16[2,3456,384]{2,1,0:T(8,128)(2,1)}, f32[80,128]{1,0:T(8,128)}) custom-call(s32[2]{0:T(128)} %lengths.5, s32[32]{0:T(128)} %order.5, bf16[2,256,768]{2,1,0:T(8,128)(2,1)} %tok.3, f32[2,256,768]{2,1,0:T(8,128)} %get-tuple-element.72.fg, ...), custom_call_target="tpu_custom_call" | custom-call | flops 80499998720 | bytes 1048576 | tf_op jit(solution)/shard_map/finish/pallas_call | solution.py:1717
  350.8 0.0 copy-start.1
  350.8 9.2 %unpack.1 = (f32[384,768]{1,0:T(8,128)}, f32[384,768]{1,0:T(8,128)}, f32[384,768]{1,0:T(8,128)}, f32[384,768]{1,0:T(8,128)}, f32[384,3072]{1,0:T(8,128)}, /*inde...) custom-call(bf16[2,3,1152,128]{3,2,1,0:T(8,128)(2,1)} %get-tuple-ele, ...), custom_call_target="tpu_custom_call" | custom-call | flops 11500000256 | bytes 1048576 | tf_op jit(solution)/shard_map/unpack/pallas_call | solution.py:1800
  360.0 0.0 copy-start
  360.0 0.0 copy-done.1
  360.0 0.9 copy.39
  360.9 0.8 copy-done
  361.7 1.1 copy.40
Async XLA Ops:
  350.8 9.2 %copy-start.1 = (bf16[2,256,768]{2,1,0:T(8,128)(2,1)S(1)}, bf16[2,256,768]{2,1,0:T(8,128)(2,1)}, u32[]{:S(2)}) copy-start(bf16[2,256,768]{2,1,0:T(8,128)(2,1)} %get-tuple-element.130) | copy-start | bytes 2359300
  360.0 1.7 copy-start

commit v3 on v2

--- a/solution.py
+++ b/solution.py
@@ -1257,7 +1257,7 @@
     out, fg, sums, wide_sums = outs
     rows = att.shape[0]
     hidden = wi.shape[1]
-    tile = 512
+    tile = 768
     rs = slice(s * rows, (s + 1) * rows)
     half = tok.shape[2] // 2
     out_bias, gain_one, shift_one, outer_bias, gain_two, shift_two = (
@@ -1750,9 +1750,15 @@
     )(lengths, order, tok, fg, rq, rkv, sums, wide_sums, ready, wq, wk, wv, others)
 
 
-def unpack_kernel(qkv, total, small, *refs):
-    outs, rows, loss, refs = refs[:6], refs[6:15], refs[15], refs[16:]
-    narrow, inner, outer, sems = refs
+def unpack_kernel(qkv_in, total_in, small, rows_in, tokens_in, *refs):
+    outs, moved, rows, loss, refs = refs[:6], refs[6:8], refs[8:17], refs[17], refs[18:]
+    qkv, total, narrow, inner, outer, sems, in_sems = refs
+    loads = [
+        pltpu.make_async_copy(src, dst, in_sems.at[i])
+        for i, (src, dst) in enumerate(((total_in, total), (qkv_in, qkv)))
+    ]
+    for copy in loads:
+        copy.start()
     half = qkv.shape[2] // 3
     blocks = inner.shape[1] // (2 * half)
     copies = []
@@ -1762,6 +1768,7 @@
         copy.start()
         copies.append(copy)
 
+    loads[0].wait()
     for k in range(2):
         cols = slice(k * half, (k + 1) * half)
         outer[:, cols] = total[k, (1 + blocks) * half :].astype(F32)
@@ -1771,6 +1778,11 @@
             cols = slice((2 * t + k) * half, (2 * t + k + 1) * half)
             inner[:, cols] = total[k, (1 + t) * half : (2 + t) * half].astype(F32)
     leave(inner, 4)
+    for i, (src, dst) in enumerate(zip((rows_in, tokens_in), moved)):
+        copy = pltpu.make_async_copy(src, dst, sems.at[6 + i])
+        copy.start()
+        copies.append(copy)
+    loads[1].wait()
     for i in range(3):
         for k in range(2):
             for p in range(3):
@@ -1794,7 +1806,7 @@
         copy.wait()
 
 
-def unpack(qkv, total, small, hidden):
+def unpack(qkv, total, small, output, tokens_grad, hidden):
     half = total.shape[2]
     narrow = jax.ShapeDtypeStruct((half, 2 * half), F32)
     return pl.pallas_call(
@@ -1803,21 +1815,26 @@
         + [
             jax.ShapeDtypeStruct((half, hidden), F32),
             jax.ShapeDtypeStruct((hidden // 2, 2 * half), F32),
+            jax.ShapeDtypeStruct(output.shape, BF16),
+            jax.ShapeDtypeStruct(tokens_grad.shape, F32),
         ]
         + [jax.ShapeDtypeStruct((half,), F32)] * 8
         + [jax.ShapeDtypeStruct((hidden // 2,), F32), jax.ShapeDtypeStruct((1, 1), F32)],
-        in_specs=[VMEM] * 3,
-        out_specs=[ANY] * 6 + [VMEM] * 10,
+        in_specs=[ANY, ANY, VMEM, ANY, ANY],
+        out_specs=[ANY] * 8 + [VMEM] * 10,
         scratch_shapes=[
+            pltpu.VMEM(qkv.shape, BF16),
+            pltpu.VMEM(total.shape, BF16),
             pltpu.VMEM((4, half, 2 * half), F32),
             pltpu.VMEM((half, hidden), F32),
             pltpu.VMEM((hidden // 2, 2 * half), F32),
-            pltpu.SemaphoreType.DMA((6,)),
+            pltpu.SemaphoreType.DMA((8,)),
+            pltpu.SemaphoreType.DMA((2,)),
         ],
         compiler_params=ROOM,
         cost_estimate=cost(10),
         name="unpack",
-    )(qkv, total, small)
+    )(qkv, total, small, output, tokens_grad)
 
 
 def pick(table, index):
@@ -2057,10 +2074,11 @@
             value_weight,
             others,
         )
-        grads = unpack(qkv, total, small, hidden)
+        grads = unpack(qkv, total, small, output, tokens_grad, hidden)
         query_grad, key_grad, value_grad, out_grad, inner_grad, outer_grad = grads[:6]
-        rows_of = dict(zip((0, 1, 2, 3, 4, 5, 7, 8, 9), grads[6:15]))
-        loss = grads[15].reshape(())
+        output, tokens_grad = grads[6:8]
+        rows_of = dict(zip((0, 1, 2, 3, 4, 5, 7, 8, 9), grads[8:17]))
+        loss = grads[17].reshape(())
 
         def vector(start, length):
             return rows_of[start // width]

time: 366 us -> 429 us (1.17)
  Pallas kernels: 359 us -> 425 us
    pallas_call x1, Pallas kernels: 9.19 us -> 77.2 us  [unpack(): pl.pallas_call(unpack_kernel, out_shape=[narrow] * 4 + [jax.ShapeDtypeStr...]
where the time goes in v3:
time: 429 us; the launch traced here: 426 us
  Pallas kernels  425 us (99%)
    pallas_call x1, Pallas kernels, attend_back_all(): pl.pallas_call(functools.partial(back_kernel, seqs), out_shape=[jax.Shape...  119 us
    pallas_call x1, Pallas kernels, start(): pl.pallas_call(functools.partial(start_kernel, seqs), out_shape=[narrow]...  106 us
    pallas_call x1, Pallas kernels, finish(): pl.pallas_call(functools.partial(finish_kernel, seqs), out_shape=[jax.Sha...  77.5 us
    pallas_call x1, Pallas kernels, unpack(): pl.pallas_call(unpack_kernel, out_shape=[narrow] * 4 + [jax.ShapeDtypeStr...  77.2 us
    pallas_call x1, Pallas kernels, middle(): pl.pallas_call(functools.partial(middle_kernel, seqs), out_shape=[jax.Sha...  45 us

profile of v3, /device:TPU:0, one launch (start us, length us, event | category | flops | bytes accessed | tf_op | source)
XLA Modules:
  0.0 425.6 jit_solution(9271237189794261614)
XLA Ops:
  0.7 105.8 %start.1 = (bf16[4,256,192]{2,1,0:T(8,128)(2,1)}, bf16[4,256,192]{2,1,0:T(8,128)(2,1)}, bf16[4,4,256,384]{3,2,1,0:T(8,128)(2,1)}, bf16[4,4,256,384]{3,2,1,0:T(8,...) custom-call(s32[2]{0:T(128)} %lengths.5, ...), custom_call_target="tpu_custom_call" | custom-call | flops 92000002048 | bytes 1048576 | tf_op jit(solution)/shard_map/start/pallas_call | solution.py:1202
  106.5 45.0 %middle.1 = (bf16[2,256,768]{2,1,0:T(8,128)(2,1)}, f32[2,256,768]{2,1,0:T(8,128)}, f32[8,768]{1,0:T(8,128)}, f32[1,3072]{1,0:T(1,128)}, bf16[1664,384]{1,0:T(8,1...) custom-call(s32[2]{0:T(128)} %lengths.5, ...), custom_call_target="tpu_custom_call" | custom-call | flops 69000003584 | bytes 1048576 | tf_op jit(solution)/shard_map/middle/pallas_call | solution.py:1445
  151.4 119.2 %attend_back_all.1 = (bf16[3,4,256,128]{3,2,1,0:T(8,128)(2,1)}, bf16[6,4,256,128]{3,2,1,0:T(8,128)(2,1)}, bf16[432,384]{1,0:T(8,128)(2,1)}) custom-call(bf16[1024,192]{1,0:T(8,128)(2,1)} %bitcast.11, bf16[1024,192]{1,0:T(8,128)(2,1)} %bitcast.15, bf16[1024,192]{1,0:T(8,128)(2,1)} %bitcast.13, f32[3,8,1024]{2,1,0:T(8,128)} %get-tuple-element.77.refs_3_, ...), custom_call_target="tpu_custom_call" | custom-call | flops 138000007168 | bytes 1048576 | tf_op jit(solution)/shard_map/attend_back_all/pallas_call | solution.py:868
  270.6 77.5 %finish.1 = (f32[2,256,768]{2,1,0:T(8,128)}, bf16[2,3,1152,128]{3,2,1,0:T(8,128)(2,1)}, bf16[2,3456,384]{2,1,0:T(8,128)(2,1)}, f32[80,128]{1,0:T(8,128)}) custom-call(s32[2]{0:T(128)} %lengths.5, s32[32]{0:T(128)} %order.5, bf16[2,256,768]{2,1,0:T(8,128)(2,1)} %tok.3, f32[2,256,768]{2,1,0:T(8,128)} %get-tuple-element.73.fg, ...), custom_call_target="tpu_custom_call" | custom-call | flops 80499998720 | bytes 1048576 | tf_op jit(solution)/shard_map/finish/pallas_call | solution.py:1717
  348.1 77.2 %unpack.1 = (f32[384,768]{1,0:T(8,128)}, f32[384,768]{1,0:T(8,128)}, f32[384,768]{1,0:T(8,128)}, f32[384,768]{1,0:T(8,128)}, f32[384,3072]{1,0:T(8,128)}, /*inde...) custom-call(bf16[2,3,1152,128]{3,2,1,0:T(8,128)(2,1)} %get-tuple-ele, ...), custom_call_target="tpu_custom_call" | custom-call | flops 11500000256 | bytes 1048576 | tf_op jit(solution)/shard_map/unpack/pallas_call | solution.py:1812

commit v4 on v3

--- a/solution.py
+++ b/solution.py
@@ -1752,10 +1752,12 @@
 
 def unpack_kernel(qkv_in, total_in, small, rows_in, tokens_in, *refs):
     outs, moved, rows, loss, refs = refs[:6], refs[6:8], refs[8:17], refs[17], refs[18:]
-    qkv, total, narrow, inner, outer, sems, in_sems = refs
+    qkv, total, rows_v, tokens_v, narrow, inner, outer, sems, in_sems = refs
     loads = [
         pltpu.make_async_copy(src, dst, in_sems.at[i])
-        for i, (src, dst) in enumerate(((total_in, total), (qkv_in, qkv)))
+        for i, (src, dst) in enumerate(
+            ((total_in, total), (qkv_in, qkv), (rows_in, rows_v), (tokens_in, tokens_v))
+        )
     ]
     for copy in loads:
         copy.start()
@@ -1778,7 +1780,8 @@
             cols = slice((2 * t + k) * half, (2 * t + k + 1) * half)
             inner[:, cols] = total[k, (1 + t) * half : (2 + t) * half].astype(F32)
     leave(inner, 4)
-    for i, (src, dst) in enumerate(zip((rows_in, tokens_in), moved)):
+    for i, (src, dst) in enumerate(zip((rows_v, tokens_v), moved)):
+        loads[2 + i].wait()
         copy = pltpu.make_async_copy(src, dst, sems.at[6 + i])
         copy.start()
         copies.append(copy)
@@ -1825,11 +1828,13 @@
         scratch_shapes=[
             pltpu.VMEM(qkv.shape, BF16),
             pltpu.VMEM(total.shape, BF16),
+            pltpu.VMEM(output.shape, BF16),
+            pltpu.VMEM(tokens_grad.shape, F32),
             pltpu.VMEM((4, half, 2 * half), F32),
             pltpu.VMEM((half, hidden), F32),
             pltpu.VMEM((hidden // 2, 2 * half), F32),
             pltpu.SemaphoreType.DMA((8,)),
-            pltpu.SemaphoreType.DMA((2,)),
+            pltpu.SemaphoreType.DMA((4,)),
         ],
         compiler_params=ROOM,
         cost_estimate=cost(10),

time: 429 us -> 361 us (0.84)
  Pallas kernels: 425 us -> 358 us
    pallas_call x1, Pallas kernels: 77.2 us -> 10.1 us  [unpack(): pl.pallas_call(unpack_kernel, out_shape=[narrow] * 4 + [jax.ShapeDtypeStr...]
where the time goes in v4:
time: 361 us; the launch traced here: 358 us
  Pallas kernels  358 us (99%)
    pallas_call x1, Pallas kernels, attend_back_all(): pl.pallas_call(functools.partial(back_kernel, seqs), out_shape=[jax.Shape...  119 us
    pallas_call x1, Pallas kernels, start(): pl.pallas_call(functools.partial(start_kernel, seqs), out_shape=[narrow]...  106 us
    pallas_call x1, Pallas kernels, finish(): pl.pallas_call(functools.partial(finish_kernel, seqs), out_shape=[jax.Sha...  77.5 us
    pallas_call x1, Pallas kernels, middle(): pl.pallas_call(functools.partial(middle_kernel, seqs), out_shape=[jax.Sha...  45 us
    pallas_call x1, Pallas kernels, unpack(): pl.pallas_call(unpack_kernel, out_shape=[narrow] * 4 + [jax.ShapeDtypeStr...  10.1 us

profile of v4, /device:TPU:0, one launch (start us, length us, event | category | flops | bytes accessed | tf_op | source)
XLA Modules:
  0.0 358.5 jit_solution(346227232970063534)
XLA Ops:
  0.7 105.8 %start.1 = (bf16[4,256,192]{2,1,0:T(8,128)(2,1)}, bf16[4,256,192]{2,1,0:T(8,128)(2,1)}, bf16[4,4,256,384]{3,2,1,0:T(8,128)(2,1)}, bf16[4,4,256,384]{3,2,1,0:T(8,...) custom-call(s32[2]{0:T(128)} %lengths.5, ...), custom_call_target="tpu_custom_call" | custom-call | flops 92000002048 | bytes 1048576 | tf_op jit(solution)/shard_map/start/pallas_call | solution.py:1202
  106.5 45.0 %middle.1 = (bf16[2,256,768]{2,1,0:T(8,128)(2,1)}, f32[2,256,768]{2,1,0:T(8,128)}, f32[8,768]{1,0:T(8,128)}, f32[1,3072]{1,0:T(1,128)}, bf16[1664,384]{1,0:T(8,1...) custom-call(s32[2]{0:T(128)} %lengths.5, ...), custom_call_target="tpu_custom_call" | custom-call | flops 69000003584 | bytes 1048576 | tf_op jit(solution)/shard_map/middle/pallas_call | solution.py:1445
  151.4 119.2 %attend_back_all.1 = (bf16[3,4,256,128]{3,2,1,0:T(8,128)(2,1)}, bf16[6,4,256,128]{3,2,1,0:T(8,128)(2,1)}, bf16[432,384]{1,0:T(8,128)(2,1)}) custom-call(bf16[1024,192]{1,0:T(8,128)(2,1)} %bitcast.11, bf16[1024,192]{1,0:T(8,128)(2,1)} %bitcast.15, bf16[1024,192]{1,0:T(8,128)(2,1)} %bitcast.13, f32[3,8,1024]{2,1,0:T(8,128)} %get-tuple-element.77.refs_3_, ...), custom_call_target="tpu_custom_call" | custom-call | flops 138000007168 | bytes 1048576 | tf_op jit(solution)/shard_map/attend_back_all/pallas_call | solution.py:868
  270.6 77.5 %finish.1 = (f32[2,256,768]{2,1,0:T(8,128)}, bf16[2,3,1152,128]{3,2,1,0:T(8,128)(2,1)}, bf16[2,3456,384]{2,1,0:T(8,128)(2,1)}, f32[80,128]{1,0:T(8,128)}) custom-call(s32[2]{0:T(128)} %lengths.5, s32[32]{0:T(128)} %order.5, bf16[2,256,768]{2,1,0:T(8,128)(2,1)} %tok.3, f32[2,256,768]{2,1,0:T(8,128)} %get-tuple-element.73.fg, ...), custom_call_target="tpu_custom_call" | custom-call | flops 80499998720 | bytes 1048576 | tf_op jit(solution)/shard_map/finish/pallas_call | solution.py:1717
  348.1 10.1 %unpack.1 = (f32[384,768]{1,0:T(8,128)}, f32[384,768]{1,0:T(8,128)}, f32[384,768]{1,0:T(8,128)}, f32[384,768]{1,0:T(8,128)}, f32[384,3072]{1,0:T(8,128)}, /*inde...) custom-call(bf16[2,3,1152,128]{3,2,1,0:T(8,128)(2,1)} %get-tuple-ele, ...), custom_call_target="tpu_custom_call" | custom-call | flops 11500000256 | bytes 1048576 | tf_op jit(solution)/shard_map/unpack/pallas_call | solution.py:1815
